TPU v7x, 512 devices: a whole 4x4x16 slice. The times are simulated.
512 devices in a mesh: dom: 128 (over y, z, core), rep: 4 (over x).
Axes of the slice: x: 4, y: 4, z: 16, core: 2. Of those that a mesh axis runs over, the one named last changes fastest.
Arguments:
- entity: bfloat16 [128, 512, 400], P(None, 'dom'), may hold values from -4 to 4
- relation: bfloat16 [2000, 400], replicated, may hold values from -3 to 3
- head_ids: int32 [512000], P(('dom', 'rep')), may hold values from 0 to 511
- relation_ids: int32 [512000], P(('dom', 'rep')), may hold values from 0 to 1999
- tail_ids: int32 [512000], P(('dom', 'rep')), may hold values from 0 to 511
- negative_ids: int32 [512, 1000], P(('dom', 'rep')), may hold values from 0 to 511
- span_counts: int32 [512], P(('dom', 'rep')), may hold values from 1 to 1000, 358400 in all
- plan: int32 [128, 2], replicated, may hold values from 0 to 127
Outputs:
- entity_grad: bfloat16 [128, 512, 400], P(None, ('dom', 'rep'))
- relation_grad: bfloat16 [2000, 400], replicated
Inputs may be any that keep to these rules, and one draw needn't show every extreme that they name: `span_counts`: some span is full. `plan`: uneven: a partition may serve several buckets or none.
All inputs are finite; a program needn't handle non-finite values. No bound on the sum of `span_counts` on one device may be relied on, other than what follows from the above.
Results may differ from a plain program's by a relative error of at most 0.014.
Values may be sent and summed in bfloat16 or wider, within the bound.
A program may use at most 64 MiB of HBM per device.

v0:
```python
import jax
import jax.numpy as jnp
from jax import lax
from jax.sharding import PartitionSpec as P


def edge_grads(head_rows, relation_rows, tail_rows, noise_rows, valid_mask):
    half_width = head_rows.shape[1] // 2
    head_full = head_rows.astype(jnp.float32)
    relation_full = relation_rows.astype(jnp.float32)
    tail_full = tail_rows.astype(jnp.float32)
    head_real, head_imag = (head_full[:, :half_width], head_full[:, half_width:])
    relation_real, relation_imag = (relation_full[:, :half_width], relation_full[:, half_width:])
    queries = jnp.concatenate(
        [
            head_real * relation_real - head_imag * relation_imag,
            head_real * relation_imag + head_imag * relation_real,
        ],
        axis=1,
    )
    queries_low = queries.astype(jnp.bfloat16)
    positive = jnp.sum(queries * tail_full, axis=1)
    negative = lax.dot_general(
        queries_low, noise_rows, (((1,), (1,)), ((), ())), preferred_element_type=jnp.float32
    )
    peak_score = jnp.maximum(jnp.max(negative, axis=1), positive)
    positive_exp = jnp.exp(positive - peak_score)
    negative_exp = jnp.exp(negative - peak_score[:, None])
    denominator = positive_exp + jnp.sum(negative_exp, axis=1)
    positive_grad = valid_mask * (positive_exp / denominator - 1.0)
    negative_grad = (negative_exp * (valid_mask / denominator)[:, None]).astype(jnp.bfloat16)
    queries_grad = positive_grad[:, None] * tail_full + jnp.dot(
        negative_grad, noise_rows, preferred_element_type=jnp.float32
    )
    tail_grad = positive_grad[:, None] * queries
    noise_grad = lax.dot_general(
        negative_grad, queries_low, (((0,), (0,)), ((), ())), preferred_element_type=jnp.float32
    )
    grad_real, grad_imag = (queries_grad[:, :half_width], queries_grad[:, half_width:])
    head_grad = jnp.concatenate(
        [
            grad_real * relation_real + grad_imag * relation_imag,
            -grad_real * relation_imag + grad_imag * relation_real,
        ],
        axis=1,
    )
    relation_grad = jnp.concatenate(
        [
            grad_real * head_real + grad_imag * head_imag,
            -grad_real * head_imag + grad_imag * head_real,
        ],
        axis=1,
    )
    return (head_grad, relation_grad, tail_grad, noise_grad)


def per_device(entity, relation, head_ids, relation_ids, tail_ids, negative_ids, span_counts, plan):
    part_count, stripe, full_width = entity.shape
    row_count = part_count * stripe
    rel_count = relation.shape[0]
    head_part = plan[:, 0]
    tail_part = plan[:, 1]
    send_head = jnp.take(entity, head_part, axis=0)
    send_tail = jnp.take(entity, tail_part, axis=0)
    got_head, got_tail = (
        lax.all_to_all(send_head, "dom", split_axis=0, concat_axis=0, tiled=True),
        lax.all_to_all(send_tail, "dom", split_axis=0, concat_axis=0, tiled=True),
    )
    head_block = got_head.reshape(row_count, full_width)
    tail_block = got_tail.reshape(row_count, full_width)
    noise_local = negative_ids[0]
    valid_mask = (jnp.arange(head_ids.shape[0], dtype=jnp.int32) < span_counts[0]).astype(
        jnp.float32
    )
    head_grad, relation_grad, tail_grad, noise_grad = edge_grads(
        head_block[head_ids],
        relation[relation_ids],
        tail_block[tail_ids],
        tail_block[noise_local],
        valid_mask,
    )
    head_sum = jax.ops.segment_sum(head_grad, head_ids, num_segments=row_count)
    tail_sum = jax.ops.segment_sum(
        tail_grad, tail_ids, num_segments=row_count
    ) + jax.ops.segment_sum(noise_grad, noise_local, num_segments=row_count)
    relation_sum = jax.ops.segment_sum(relation_grad, relation_ids, num_segments=rel_count)
    head_three = head_sum.reshape(part_count, stripe, full_width)
    tail_three = tail_sum.reshape(part_count, stripe, full_width)
    owners = jnp.arange(part_count, dtype=jnp.int32)
    pick_head = (head_part[None, :] == owners[:, None]).astype(jnp.float32)
    pick_tail = (tail_part[None, :] == owners[:, None]).astype(jnp.float32)
    back_head, back_tail = (
        lax.all_to_all(head_three, "dom", split_axis=0, concat_axis=0, tiled=True),
        lax.all_to_all(tail_three, "dom", split_axis=0, concat_axis=0, tiled=True),
    )
    flat_width = back_head.shape[1] * back_head.shape[2]
    totals = jnp.dot(
        pick_head,
        back_head.reshape(part_count, flat_width),
        precision=lax.Precision.HIGHEST,
        preferred_element_type=jnp.float32,
    ) + jnp.dot(
        pick_tail,
        back_tail.reshape(part_count, flat_width),
        precision=lax.Precision.HIGHEST,
        preferred_element_type=jnp.float32,
    )
    entity_total = lax.psum_scatter(
        totals.reshape(back_head.shape).astype(jnp.bfloat16), "rep", scatter_dimension=1, tiled=True
    )
    relation_total = lax.psum(relation_sum, ("dom", "rep"))
    return (entity_total, relation_total.astype(jnp.bfloat16))


def solution(mesh):
    placed = (
        P(None, "dom", None),
        P(),
        P(("dom", "rep")),
        P(("dom", "rep")),
        P(("dom", "rep")),
        P(("dom", "rep"), None),
        P(("dom", "rep")),
        P(),
    )
    return jax.shard_map(
        per_device,
        mesh=mesh,
        in_specs=placed,
        out_specs=(P(None, ("dom", "rep"), None), P()),
        check_vma=False,
    )
```

profile of v0, /device:TPU:1, one launch (start us, length us, event | category | flops | bytes accessed | tf_op | source)
XLA Modules:
  0.0 459.9 jit_solution(16509138429812471981)
XLA Ops:
  7.2 0.8 compare_and_fusion.1
  7.9 1.4 copy.16
  9.3 1.0 gather_fusion.4
  10.4 1.1 broadcast_select_fusion.1
  11.5 20.6 %all-to-all-start = ((bf16[128,4,400]{2,1,0:T(4,128)(2,1)}), bf16[128,4,400]{2,1,0:T(4,128)(2,1)S(1)}, u32[]{:S(2)}, u32[]{:S(2)}) async-start(bf16[128,4,400]{2,1,0:T(4,128)(2,1)} %broadcast_select_fusion.1), calls=%async_computation | async-start | bytes 1048576 | tf_op jit(solution)/shard_map/all_to_all | solution.py:66
  32.1 1.0 gather_fusion.5
  33.1 1.1 broadcast_select_fusion
  34.3 31.0 %all-to-all-done = bf16[128,4,400]{2,1,0:T(4,128)(2,1)S(1)} async-done(((bf16[128,4,400]{2,1,0:T(4,128)(2,1)}), bf16[128,4,400]{2,1,0:T(4,128)(2,1)S(1)}, u32[]{:S(2)}, u32[]{:S(2)}) %all-to-all-start) | async-done | bytes 409632 | tf_op jit(solution)/shard_map/all_to_all | solution.py:66
  65.3 8.0 %all-to-all-start.1 = ((bf16[128,4,400]{2,1,0:T(4,128)(2,1)}), bf16[128,4,400]{2,1,0:T(4,128)(2,1)}, u32[]{:S(2)}, u32[]{:S(2)}) async-start(bf16[128,4,400]{2,1,0:T(4,128)(2,1)} %broadcast_select_fusion), calls=%async_computation.1 | async-start | bytes 1048576 | tf_op jit(solution)/shard_map/all_to_all | solution.py:67
  74.0 2.9 copy.18
  76.9 4.1 gather_fusion.1
  81.0 1.4 copy.19
  82.4 1.4 convert_element_type.34
  84.2 4.1 gather_fusion
  88.3 1.4 copy.17
  89.7 2.5 convert_element_type.33
  92.2 13.8 %all-to-all-done.1 = bf16[128,4,400]{2,1,0:T(4,128)(2,1)} async-done(((bf16[128,4,400]{2,1,0:T(4,128)(2,1)}), bf16[128,4,400]{2,1,0:T(4,128)(2,1)}, u32[]{:S(2)}, u32[]{:S(2)}) %all-to-all-start.1) | async-done | bytes 409632 | tf_op jit(solution)/shard_map/all_to_all | solution.py:67
  106.0 1.3 reshape.91
  107.3 5.1 %gather_fusion.3 = bf16[1000,400]{1,0:T(8,128)(2,1)} fusion(bf16[512,400]{1,0:T(8,128)(2,1)S(1)} %reshape.91, s32[1024]{0:T(1024)S(1)} %pad_clamp_fusion), kind=kCustom, calls=%fused_computation.5 | custom fusion | bytes 1604000 | tf_op jit(solution)/shard_map/gather | solution.py:79
  112.3 5.1 %gather_fusion.2 = bf16[1000,400]{1,0:T(8,128)(2,1)} fusion(bf16[512,400]{1,0:T(8,128)(2,1)S(1)} %reshape.91, s32[1024]{0:T(1024)S(1)} %pad_clamp_fusion.1), kind=kCustom, calls=%fused_computation.4 | custom fusion | bytes 1604000 | tf_op jit(solution)/shard_map/gather | solution.py:78
  117.4 2.3 copy.21
  120.1 0.8 copy-done.7
  121.2 0.7 copy-done.6
  122.0 1.3 fusion.23
  123.3 0.6 fusion
  123.9 1.2 copy-done
  125.2 1.1 fusion.5
  126.3 0.9 multiply_add_fusion.1
  127.6 1.9 copy.22
  129.5 8.2 %scatter_custom_fusion = f32[512,400]{1,0:T(8,128)} fusion(s32[1000]{0:T(1024)S(1)} %copy-done.11, f32[1000,400]{1,0:T(8,128)} %copy.22, f32[]{:T(128)} %constant.2.clone.1), kind=kCustom, calls=%fused_computation.36 | custom fusion | flops 400000 | bytes 819712 | tf_op jit(solution)/shard_map/scatter-add | solution.py:82
  137.8 2.7 reshape.92
  140.4 7.8 %all-to-all-start.2 = ((f32[128,4,400]{2,1,0:T(4,128)}), f32[128,4,400]{2,1,0:T(4,128)}, u32[]{:S(2)}, u32[]{:S(2)}) async-start(f32[128,4,400]{2,1,0:T(4,128)} %reshape.92), calls=%async_computation.2 | async-start | bytes 2097152 | tf_op jit(solution)/shard_map/all_to_all | solution.py:93
  148.3 1.3 fusion.6
  149.6 2.8 copy.24
  152.4 8.2 %scatter_custom_fusion.1 = f32[512,400]{1,0:T(8,128)} fusion(s32[1000]{0:T(1024)S(1)} %copy-done.12, f32[1000,400]{1,0:T(8,128)} %copy.24, f32[]{:T(128)} %constant.2.clone.1), kind=kCustom, calls=%fused_computation.34 | custom fusion | flops 400000 | bytes 819712 | tf_op jit(solution)/shard_map/scatter-add | solution.py:83
  160.7 4.7 %fusion.14 = f32[1000,400]{1,0:T(8,128)} fusion(f32[1000,1000]{0,1:T(8,128)} %copy-done, f32[1000]{0:T(1024)S(1)} %get-tuple-element.17, f32[1000]{0:T(1024)S(1)} %max.13, f32[1000,200]{0,1:T(8,128)S(1)} %copy-done.5, f32[1000,200]{0,1:T(8,128)S(1)} %copy-done.3), kind=kOutput, calls=%fused_computation.40 | convolution fusion | flops 804600000 | bytes 7208000 | tf_op jit(solution)/shard_map/dot_general | solution.py:36
  165.4 7.5 %scatter_custom_fusion.2 = f32[512,400]{1,0:T(8,128)S(1)} fusion(s32[1000]{0:T(1024)S(1)} %bitcast.27, f32[1000,400]{1,0:T(8,128)} %fusion.14, f32[]{:T(128)} %constant.2.clone.1), kind=kCustom, calls=%fused_computation.32 | custom fusion | flops 400000 | bytes 819712 | tf_op jit(solution)/shard_map/scatter-add | solution.py:85
  172.9 2.4 add.89
  175.3 2.7 reshape.94
  178.0 24.3 %all-to-all-done.2 = f32[128,4,400]{2,1,0:T(4,128)} async-done(((f32[128,4,400]{2,1,0:T(4,128)}), f32[128,4,400]{2,1,0:T(4,128)}, u32[]{:S(2)}, u32[]{:S(2)}) %all-to-all-start.2) | async-done | bytes 819232 | tf_op jit(solution)/shard_map/all_to_all | solution.py:93
  202.2 8.5 %all-to-all-start.3 = ((f32[128,4,400]{2,1,0:T(4,128)}), f32[128,4,400]{2,1,0:T(4,128)S(1)}, u32[]{:S(2)}, u32[]{:S(2)}) async-start(f32[128,4,400]{2,1,0:T(4,128)} %reshape.94), calls=%async_computation.3 | async-start | bytes 2097152 | tf_op jit(solution)/shard_map/all_to_all | solution.py:94
  210.8 1.9 copy.27
  212.7 9.4 %scatter_custom_fusion.3 = f32[2000,400]{1,0:T(8,128)} fusion(s32[1000]{0:T(1024)S(1)} %copy-done.14, f32[1000,400]{1,0:T(8,128)} %copy.27, f32[]{:T(128)} %constant.2.clone.1), kind=kCustom, calls=%fused_computation.15 | custom fusion | flops 400000 | bytes 3200512 | tf_op jit(solution)/shard_map/scatter-add | solution.py:86
  222.1 1.6 copy.23
  224.2 40.9 %all-to-all-done.3 = f32[128,4,400]{2,1,0:T(4,128)S(1)} async-done(((f32[128,4,400]{2,1,0:T(4,128)}), f32[128,4,400]{2,1,0:T(4,128)S(1)}, u32[]{:S(2)}, u32[]{:S(2)}) %all-to-all-start.3) | async-done | bytes 819232 | tf_op jit(solution)/shard_map/all_to_all | solution.py:94
  265.5 1.3 fusion.1
  266.8 183.6 %all-reduce.1 = bf16[2000,400]{1,0:T(8,128)(2,1)S(1)} all-reduce(f32[2000,400]{1,0:T(8,128)} %scatter_custom_fusion.3), channel_id=1, replica_groups=mesh['dom'=128,'rep'=4] {'dom','rep'}, use_global_device_ids=true, to_apply=%region_8.10 | all-reduce | flops 800000 | bytes 4800000 | tf_op jit(solution)/shard_map/psum | solution.py:111
  450.4 2.2 copy.28
  (49 shorter events, 2.5 us)
Async XLA Ops:
  11.5 53.8 %all-to-all-start = ((bf16[128,4,400]{2,1,0:T(4,128)(2,1)}), bf16[128,4,400]{2,1,0:T(4,128)(2,1)S(1)}, u32[]{:S(2)}, u32[]{:S(2)}) async-start(bf16[128,4,400]{2,1,0:T(4,128)(2,1)} %broadcast_select_fusion.1), calls=%async_computation | async-start | bytes 1048576 | tf_op jit(solution)/shard_map/all_to_all | solution.py:66
  65.3 8.0 %copy-start.8 = (bf16[128,4,400]{2,1,0:T(4,128)(2,1)}, bf16[128,4,400]{2,1,0:T(4,128)(2,1)S(1)}, u32[]{:S(2)}) copy-start(bf16[128,4,400]{2,1,0:T(4,128)(2,1)S(1)} %all-to-all-done) | copy-start | bytes 1228804
  65.3 40.7 %all-to-all-start.1 = ((bf16[128,4,400]{2,1,0:T(4,128)(2,1)}), bf16[128,4,400]{2,1,0:T(4,128)(2,1)}, u32[]{:S(2)}, u32[]{:S(2)}) async-start(bf16[128,4,400]{2,1,0:T(4,128)(2,1)} %broadcast_select_fusion), calls=%async_computation.1 | async-start | bytes 1048576 | tf_op jit(solution)/shard_map/all_to_all | solution.py:67
  73.3 3.6 copy-start.14
  81.0 2.8 copy-start.11
  81.0 2.8 copy-start.12
  81.0 2.9 copy-start.13
  82.4 1.5 copy-start.9
  117.4 2.3 copy-start.1
  119.7 1.1 copy-start.7
  120.1 3.2 copy-start.2
  120.1 3.2 copy-start.4
  120.1 1.9 copy-start.6
  123.2 1.9 copy-start
  137.8 10.5 %copy-start.3 = (f32[1000,200]{0,1:T(8,128)S(1)}, f32[1000,200]{0,1:T(8,128)}, u32[]{:S(2)}) copy-start(f32[1000,200]{0,1:T(8,128)} %copy-done.2) | copy-start | bytes 2400004
  137.8 10.5 %copy-start.5 = (f32[1000,200]{0,1:T(8,128)S(1)}, f32[1000,200]{0,1:T(8,128)}, u32[]{:S(2)}) copy-start(f32[1000,200]{0,1:T(8,128)} %copy-done.4) | copy-start | bytes 2400004
  140.4 61.8 %all-to-all-start.2 = ((f32[128,4,400]{2,1,0:T(4,128)}), f32[128,4,400]{2,1,0:T(4,128)}, u32[]{:S(2)}, u32[]{:S(2)}) async-start(f32[128,4,400]{2,1,0:T(4,128)} %reshape.92), calls=%async_computation.2 | async-start | bytes 2097152 | tf_op jit(solution)/shard_map/all_to_all | solution.py:93
  175.3 35.5 %copy-start.10 = (s32[128,2]{0,1:T(2,128)S(1)}, s32[128,2]{0,1:T(2,128)}, u32[]{:S(2)}) copy-start(s32[128,2]{0,1:T(2,128)} %param.17) | copy-start | bytes 3076
  202.2 62.8 %all-to-all-start.3 = ((f32[128,4,400]{2,1,0:T(4,128)}), f32[128,4,400]{2,1,0:T(4,128)S(1)}, u32[]{:S(2)}, u32[]{:S(2)}) async-start(f32[128,4,400]{2,1,0:T(4,128)} %reshape.94), calls=%async_computation.3 | async-start | bytes 2097152 | tf_op jit(solution)/shard_map/all_to_all | solution.py:94
  210.7 241.9 %reduce-scatter.2.cloned.1.call-start = ((), (), s32[]{:S(2)}) async-start(), calls=%async_computation.5 | async-start | bytes 512000 | tf_op jit(solution)/shard_map/reduce_scatter | solution.py:108
Sparse Core Ops, SparseCore 0:
  266.9 21.0 reduce-scatter.1
where the time goes:
time: 466 us; the launch traced here: 460 us
  blocking collectives  184 us (39%)
  waiting for transfers between devices  110 us (24%)
  local copies, waits for them, and re-layouts  50.4 us (11%)
  other arithmetic  46.7 us (10%)
  starting transfers between devices  44.8 us (10%)
  between operations  15.5 us (3%)
  matrix products  8.87 us (2%)
    psum x1, blocking collectives, per_device(): relation_total = lax.psum(relation_sum, ('dom', 'rep'))  184 us
    all_to_all x1, waiting for transfers between devices, per_device(): lax.all_to_all(tail_three, 'dom', split_axis=0, concat_axis=0, tiled=True)  40.9 us
    all_to_all x1, waiting for transfers between devices, per_device(): lax.all_to_all(send_head, 'dom', split_axis=0, concat_axis=0, tiled=True)  31 us
    all_to_all x1, waiting for transfers between devices, per_device(): lax.all_to_all(head_three, 'dom', split_axis=0, concat_axis=0, tiled=True)  24.3 us
    all_to_all x1, starting transfers between devices, per_device(): lax.all_to_all(send_head, 'dom', split_axis=0, concat_axis=0, tiled=True)  20.6 us
    all_to_all x1, waiting for transfers between devices, per_device(): lax.all_to_all(send_tail, 'dom', split_axis=0, concat_axis=0, tiled=True)  13.8 us
    scatter-add x1, other arithmetic, per_device(): jax.ops.segment_sum(relation_grad, relation_ids, num_segments=rel_count)  9.37 us
    unnamed x33, local copies, waits for them, and re-layouts  9.34 us
  transfers between devices with their start and end apart: 5, of which 4 were waited for; matrix products, arithmetic and copies ran while one was open for 14% of the time, Pallas kernels for 0%

commit v1 on v0

v1 whole, which is shorter than its diff:
```python
import functools

import jax
import jax.numpy as jnp
from jax import lax
from jax.experimental import pallas as pl
from jax.experimental.pallas import tpu as pltpu
from jax.sharding import PartitionSpec as P

MESH = pl.DeviceIdType.MESH
F32, BF16, I32 = jnp.float32, jnp.bfloat16, jnp.int32
VMEM = pl.BlockSpec(memory_space=pltpu.VMEM)
SMEM = pl.BlockSpec(memory_space=pltpu.SMEM)

NY, NZ, NC, NX = 4, 16, 2, 4
NYC = NY * NC
NDOM = NY * NZ * NC
D = 400
HALF = D // 2
RELS = 2000
SPAN = 1000
SLOTS = 1024
CHUNK = 256
ROWS = 512
QUART = 256
YROWS = 112
YPAD = 128
NEVER = -1e30


def nn(a, b):
    return lax.dot_general(a, b, (((1,), (0,)), ((), ())), preferred_element_type=F32)


def nt(a, b):
    return lax.dot_general(a, b, (((1,), (1,)), ((), ())), preferred_element_type=F32)


def tn(a, b):
    return lax.dot_general(a, b, (((0,), (0,)), ((), ())), preferred_element_type=F32)


def iota(shape, axis):
    return lax.broadcasted_iota(I32, shape, axis)


def onehot(hit):
    return jnp.where(hit, 1.0, 0.0).astype(BF16)


class Place:
    def __init__(self):
        dom, self.x = lax.axis_index("dom"), lax.axis_index("rep")
        self.c = lax.rem(dom, NC)
        self.z = lax.rem(lax.div(dom, NC), NZ)
        self.y = lax.div(dom, NC * NZ)
        self.yc = self.y * NC + self.c
        self.dom = dom

    def at(self, z=None, yc=None, x=None):
        z = self.z if z is None else z
        yc = self.yc if yc is None else yc
        x = self.x if x is None else x
        return {"dom": (lax.div(yc, NC) * NZ + z) * NC + lax.rem(yc, NC), "rep": x}

    def others(self, axis, body):
        size, me = {"z": (NZ, self.z), "yc": (NYC, self.yc), "x": (NX, self.x), "y": (NY, self.y)}[axis]

        def step(k, carry):
            body(lax.rem(me + k, size))
            return carry

        lax.fori_loop(1, size, step, 0)

    def barrier(self):
        sem = pltpu.get_barrier_semaphore()

        def hello(**where):
            pl.semaphore_signal(sem, inc=1, device_id=self.at(**where), device_id_type=MESH)

        self.others("x", lambda p: hello(x=p))
        self.others("yc", lambda p: hello(yc=p))
        self.others("z", lambda p: hello(z=p))
        pl.semaphore_wait(sem, NX + NYC + NZ - 3)


def remote(src, dst, send, recv, where):
    return pltpu.make_async_remote_copy(
        src_ref=src, dst_ref=dst, send_sem=send, recv_sem=recv, device_id=where, device_id_type=MESH
    )


def worker_major(shape, row_axis):
    row, col = iota(shape, row_axis), iota(shape, 1 - row_axis)
    half = lax.bitwise_and(row, 1)
    core = lax.bitwise_and(lax.shift_right_logical(row, 1), 1)
    y = lax.bitwise_and(lax.shift_right_logical(row, 2), 3)
    z = lax.shift_right_logical(row, 4)
    return onehot(col == half * NDOM + (y * NZ + z) * NC + core)


def swap_zy(shape, row_axis):
    row, col = iota(shape, row_axis), iota(shape, 1 - row_axis)
    half = lax.bitwise_and(row, 1)
    z = lax.bitwise_and(lax.shift_right_logical(row, 1), 15)
    yc = lax.shift_right_logical(row, 5)
    return onehot(col == z * 16 + yc * 2 + half)


def gather_kernel(ent, plan, out, snd1, rcv1, snd2, rcv2, s1, r1, s2, r2, s3, r3):
    me = Place()
    me.barrier()
    stripe = ent[me.x]
    sq = (NDOM, NDOM)
    picked = [nn(stripe, onehot(iota(sq, 0) == plan[h : h + 1, :])).astype(BF16) for h in range(2)]
    wide = jnp.concatenate(picked, axis=1)
    mat = (2 * NDOM, 2 * NDOM)
    snd1[...] = nt(worker_major(mat, 0), wide).astype(BF16).reshape(snd1.shape)

    def copy1(dst, src):
        return remote(snd1.at[dst], rcv1.at[src], s1.at[dst], r1.at[src], me.at(z=dst))

    me.others("z", lambda p: copy1(p, me.z).start())
    rcv1[me.z] = snd1[me.z]
    me.others("z", lambda p: copy1(p, p).wait_recv())
    snd2[...] = nn(swap_zy(mat, 0), rcv1[...].reshape(2 * NDOM, D)).astype(BF16).reshape(snd2.shape)

    def copy2(dst, src):
        return remote(snd2.at[dst], rcv2.at[src], s2.at[dst], r2.at[src], me.at(yc=dst))

    me.others("yc", lambda p: copy2(p, me.yc).start())
    rcv2[me.yc] = snd2[me.yc]
    me.others("yc", lambda p: copy2(p, p).wait_recv())
    row, col = iota(mat, 0), iota(mat, 1)
    half = lax.bitwise_and(row, 1)
    z = lax.bitwise_and(lax.shift_right_logical(row, 1), 15)
    yc = lax.shift_right_logical(row, 5)
    owner = (lax.shift_right_logical(yc, 1) * NZ + z) * NC + lax.bitwise_and(yc, 1)
    back = onehot(col == half * NDOM + owner)
    out[me.x] = tn(rcv2[...].reshape(2 * NDOM, D), back).astype(BF16)

    def copy3(dst, src):
        return remote(out.at[src], out.at[src], s3.at[dst], r3.at[src], me.at(x=dst))

    me.others("x", lambda p: copy3(p, me.x).start())
    me.others("x", lambda p: copy3(p, p).wait_recv())
    me.others("z", lambda p: copy1(p, me.z).wait_send())
    me.others("yc", lambda p: copy2(p, me.yc).wait_send())
    me.others("x", lambda p: copy3(p, me.x).wait_send())


def gather(ent, plan):
    dma = pltpu.SemaphoreType.DMA
    return pl.pallas_call(
        gather_kernel,
        out_shape=jax.ShapeDtypeStruct((NX, D, 2 * NDOM), BF16),
        in_specs=[VMEM, VMEM],
        out_specs=VMEM,
        scratch_shapes=[
            pltpu.VMEM((NZ, 2 * NYC, D), BF16),
            pltpu.VMEM((NZ, 2 * NYC, D), BF16),
            pltpu.VMEM((NYC, 2 * NZ, D), BF16),
            pltpu.VMEM((NYC, 2 * NZ, D), BF16),
            dma((NZ,)),
            dma((NZ,)),
            dma((NYC,)),
            dma((NYC,)),
            dma((NX,)),
            dma((NX,)),
        ],
        compiler_params=pltpu.CompilerParams(
            collective_id=0, has_side_effects=True, vmem_limit_bytes=40 << 20
        ),
        name="gather_rows",
    )(ent, plan)


def span_kernel(
    got, rel, head, relid, tail, neg, count, rel_sum, ent_sum, ids, hb, tb, tr, logc, h1, r1, dr, dh, av, ql
):
    ids[...] = jnp.full(ids.shape, -4, I32)
    for k, ref in enumerate((head, relid, tail, neg)):
        ids[k : k + 1, 0:SPAN] = ref[...]
    raw = ids[...]
    place = lax.bitwise_and(raw, 3) * NDOM + lax.shift_right_arithmetic(raw, 2)
    ids[...] = jnp.where(iota(ids.shape, 0) == 1, raw, place)
    for x in range(NX):
        hb[:, x * NDOM : (x + 1) * NDOM] = got[x, :, 0:NDOM]
        tb[:, x * NDOM : (x + 1) * NDOM] = got[x, :, NDOM:]
    tr[...] = tb[...].T
    times = jnp.zeros((ROWS, 1), F32)
    for k in range(SLOTS // CHUNK):
        hit = iota((ROWS, CHUNK), 0) == ids[3:4, k * CHUNK : (k + 1) * CHUNK]
        times += jnp.sum(jnp.where(hit, 1.0, 0.0), axis=1, keepdims=True)
    logc[...] = jnp.where(times > 0.0, jnp.log(jnp.maximum(times, 1.0)), NEVER)

    def chunk(k, carry):
        at = pl.ds(pl.multiple_of(k * CHUNK, CHUNK), CHUNK)
        h1[:, at] = onehot(iota((ROWS, CHUNK), 0) == ids[0:1, at])
        r1[:, at] = onehot(iota((2048, CHUNK), 0) == ids[1:2, at])
        tail_hit = iota((ROWS, CHUNK), 0) == ids[2:3, at]
        h = nn(hb[...], h1[:, at])
        r = nn(rel[...], r1[0:RELS, at])
        t = nn(tb[...], onehot(tail_hit))
        h_re, h_im = h[0:HALF], h[HALF:D]
        r_re, r_im = r[0:HALF], r[HALF:D]
        q_re = h_re * r_re - h_im * r_im
        q_im = h_re * r_im + h_im * r_re
        s0 = jnp.sum(q_re * t[0:HALF] + q_im * t[HALF:D], axis=0, keepdims=True)
        q_low = jnp.concatenate([q_re, q_im], axis=0).astype(BF16)
        ql[:, at] = q_low
        s = nn(tr[...], q_low) + logc[...]
        m = jnp.maximum(s0, jnp.max(s, axis=0, keepdims=True))
        e0 = jnp.exp(s0 - m)
        e = jnp.exp(s - m)
        z = e0 + jnp.sum(e, axis=0, keepdims=True)
        slot = iota((1, CHUNK), 1) + k * CHUNK
        valid = jnp.where(slot < count[0], 1.0, 0.0)
        g0 = valid * (e0 / z - 1.0)
        a = (e * (valid / z) + jnp.where(tail_hit, g0, 0.0)).astype(BF16)
        av[:, at] = a
        dq = nn(tb[...], a)
        d_re, d_im = dq[0:HALF], dq[HALF:D]
        dh[:, at] = jnp.concatenate(
            [d_re * r_re + d_im * r_im, d_im * r_re - d_re * r_im], axis=0
        ).astype(BF16)
        dr[:, at] = jnp.concatenate(
            [d_re * h_re + d_im * h_im, d_im * h_re - d_re * h_im], axis=0
        ).astype(BF16)
        return carry

    lax.fori_loop(0, SLOTS // CHUNK, chunk, 0)

    def relation_block(k, carry):
        rows = pl.ds(pl.multiple_of(k * QUART, QUART), QUART)
        rel_sum[k] = nt(dr[...], r1[rows, :]).astype(BF16)
        return carry

    lax.fori_loop(0, NC * NX, relation_block, 0)

    def entity_block(x, carry):
        rows = pl.ds(pl.multiple_of(x * NDOM, NDOM), NDOM)
        ent_sum[x, :, 0:NDOM] = nt(dh[...], h1[rows, :]).astype(BF16)
        ent_sum[x, :, NDOM : 2 * NDOM] = nt(ql[...], av[rows, :]).astype(BF16)
        return carry

    lax.fori_loop(0, NX, entity_block, 0)


def span(got, rel, head, relid, tail, neg, count):
    return pl.pallas_call(
        span_kernel,
        out_shape=(
            jax.ShapeDtypeStruct((NC * NX, D, QUART), BF16),
            jax.ShapeDtypeStruct((NX, D, 2 * NDOM), BF16),
        ),
        in_specs=[VMEM] * 6 + [SMEM],
        out_specs=(VMEM, VMEM),
        scratch_shapes=[
            pltpu.VMEM((8, SLOTS), I32),
            pltpu.VMEM((D, ROWS), BF16),
            pltpu.VMEM((D, ROWS), BF16),
            pltpu.VMEM((ROWS, D), BF16),
            pltpu.VMEM((ROWS, 1), F32),
            pltpu.VMEM((ROWS, SLOTS), BF16),
            pltpu.VMEM((2048, SLOTS), BF16),
            pltpu.VMEM((D, SLOTS), BF16),
            pltpu.VMEM((D, SLOTS), BF16),
            pltpu.VMEM((ROWS, SLOTS), BF16),
            pltpu.VMEM((D, SLOTS), BF16),
        ],
        compiler_params=pltpu.CompilerParams(vmem_limit_bytes=50 << 20),
        name="span_gradients",
    )(got, rel, head, relid, tail, neg, count)


def reduce_kernel(
    rel_sum, ent_sum, plan, ent_out, rel_out,
    rc, xs, rx, ys, ry, zs, rz, agz, agy, agx, agc, rex, sb1, rb1, sb2, rb2,
    s_c, r_c, s_x, r_x, s_y, r_y, s_z, r_z, s_az, r_az, s_ay, r_ay, s_ax, r_ax, s_ac, r_ac,
    s_ex, r_ex, s_b1, r_b1, s_b2, r_b2,
):
    me = Place()
    me.barrier()
    other_core = me.at(yc=me.y * NC + (1 - me.c))

    def core_copy(j):
        return remote(rel_sum.at[(1 - me.c) * NX + j], rc.at[j], s_c.at[j], r_c.at[j], other_core)

    def x_copy(dst, src):
        return remote(xs.at[dst], rx.at[src], s_x.at[dst], r_x.at[src], me.at(x=dst))

    def ent_copy(dst, src):
        return remote(ent_sum.at[dst], rex.at[src], s_ex.at[dst], r_ex.at[src], me.at(x=dst))

    def add_core(j):
        core_copy(j).wait_recv()
        xs[j] = (rel_sum[me.c * NX + j].astype(F32) + rc[j].astype(F32)).astype(BF16)

    me.others("x", lambda p: core_copy(p).start())
    core_copy(me.x).start()

    def add_and_send(p):
        add_core(p)
        x_copy(p, me.x).start()

    me.others("x", add_and_send)
    add_core(me.x)
    me.others("x", lambda p: ent_copy(p, me.x).start())
    rx[me.x] = xs[me.x]
    me.others("x", lambda p: x_copy(p, p).wait_recv())
    total = rx[0].astype(F32) + rx[1].astype(F32) + rx[2].astype(F32) + rx[3].astype(F32)
    total = total.astype(BF16)
    for y in range(NY):
        rows = min(YROWS, D - y * YROWS)
        ys[y, 0:rows] = total[y * YROWS : y * YROWS + rows]
        if rows < YPAD:
            ys[y, rows:YPAD] = jnp.zeros((YPAD - rows, QUART), BF16)

    def y_copy(dst, src):
        return remote(ys.at[dst], ry.at[src], s_y.at[dst], r_y.at[src], me.at(yc=dst * NC + me.c))

    me.others("y", lambda p: y_copy(p, me.y).start())
    ry[me.y] = ys[me.y]
    me.others("y", lambda p: y_copy(p, p).wait_recv())
    total = ry[0].astype(F32) + ry[1].astype(F32) + ry[2].astype(F32) + ry[3].astype(F32)
    total = total.astype(BF16)
    for z in range(NZ):
        i, j = z // 2, z % 2
        zs[z] = total[i * 16 : (i + 1) * 16, j * 128 : (j + 1) * 128]

    def z_copy(dst, src):
        return remote(zs.at[dst], rz.at[src], s_z.at[dst], r_z.at[src], me.at(z=dst))

    me.others("z", lambda p: z_copy(p, me.z).start())
    rz[me.z] = zs[me.z]

    mat = (2 * NDOM, 2 * NDOM)
    rex[me.x] = ent_sum[me.x]
    me.others("x", lambda p: ent_copy(p, p).wait_recv())
    mine = rex[0].astype(F32) + rex[1].astype(F32) + rex[2].astype(F32) + rex[3].astype(F32)
    row, col = iota(mat, 0), iota(mat, 1)
    half = lax.bitwise_and(row, 1)
    z_of = lax.bitwise_and(lax.shift_right_logical(row, 1), 15)
    yc_of = lax.shift_right_logical(row, 5)
    owner = (lax.shift_right_logical(yc_of, 1) * NZ + z_of) * NC + lax.bitwise_and(yc_of, 1)
    by_owner = onehot(col == half * NDOM + owner)
    sb1[...] = nt(by_owner, mine.astype(BF16)).astype(BF16).reshape(sb1.shape)

    def b1_copy(dst, src):
        return remote(sb1.at[dst], rb1.at[src], s_b1.at[dst], r_b1.at[src], me.at(yc=dst))

    me.others("yc", lambda p: b1_copy(p, me.yc).start())
    rb1[me.yc] = sb1[me.yc]

    me.others("z", lambda p: z_copy(p, p).wait_recv())
    total = rz[0].astype(F32)
    for z in range(1, NZ):
        total += rz[z].astype(F32)
    agz[me.z] = total.astype(BF16)

    def az_copy(dst, src):
        return remote(agz.at[src], agz.at[src], s_az.at[dst], r_az.at[src], me.at(z=dst))

    me.others("z", lambda p: az_copy(p, me.z).start())

    me.others("yc", lambda p: b1_copy(p, p).wait_recv())
    sb2[...] = tn(swap_zy(mat, 0), rb1[...].reshape(2 * NDOM, D)).astype(BF16).reshape(sb2.shape)

    def b2_copy(dst, src):
        return remote(sb2.at[dst], rb2.at[src], s_b2.at[dst], r_b2.at[src], me.at(z=dst))

    me.others("z", lambda p: b2_copy(p, me.z).start())
    rb2[me.z] = sb2[me.z]

    me.others("z", lambda p: az_copy(p, p).wait_recv())
    for z in range(NZ):
        i, j = z // 2, z % 2
        agy[me.y, i * 16 : (i + 1) * 16, j * 128 : (j + 1) * 128] = agz[z]

    def ay_copy(dst, src):
        return remote(agy.at[src], agy.at[src], s_ay.at[dst], r_ay.at[src], me.at(yc=dst * NC + me.c))

    me.others("y", lambda p: ay_copy(p, me.y).start())
    me.others("y", lambda p: ay_copy(p, p).wait_recv())
    for y in range(NY):
        rows = min(YROWS, D - y * YROWS)
        agx[me.x, y * YROWS : y * YROWS + rows] = agy[y, 0:rows]

    def ax_copy(dst, src):
        return remote(agx.at[src], agx.at[src], s_ax.at[dst], r_ax.at[src], me.at(x=dst))

    def ac_copy(j):
        return remote(agx.at[j], agc.at[j], s_ac.at[j], r_ac.at[j], other_core)

    me.others("x", lambda p: ax_copy(p, me.x).start())
    ac_copy(me.x).start()

    def pass_on(p):
        ax_copy(p, p).wait_recv()
        ac_copy(p).start()

    me.others("x", pass_on)

    plan_hit = jnp.concatenate(
        [onehot(iota((NDOM, NDOM), 0) == plan[h : h + 1, :]) for h in range(2)], axis=1
    )
    pick = nt(worker_major(mat, 0), plan_hit).astype(BF16)
    me.others("z", lambda p: b2_copy(p, p).wait_recv())
    ent_out[...] = tn(rb2[...].reshape(2 * NDOM, D), pick).astype(BF16)

    me.others("x", lambda p: ac_copy(p).wait_recv())
    ac_copy(me.x).wait_recv()
    first = me.c == 0
    for j in range(NX):
        low = jnp.where(first, agx[j].astype(F32), agc[j].astype(F32)).astype(BF16)
        high = jnp.where(first, agc[j].astype(F32), agx[j].astype(F32)).astype(BF16)
        rel_out[:, j * QUART : (j + 1) * QUART] = low
        start = (NX + j) * QUART
        width = min(QUART, RELS - start)
        rel_out[:, start : start + width] = high[:, 0:width]

    core_copy(me.x).wait_send()
    ac_copy(me.x).wait_send()
    for act in (
        lambda p: core_copy(p).wait_send(),
        lambda p: x_copy(p, me.x).wait_send(),
        lambda p: ent_copy(p, me.x).wait_send(),
        lambda p: ax_copy(p, me.x).wait_send(),
        lambda p: ac_copy(p).wait_send(),
    ):
        me.others("x", act)
    me.others("y", lambda p: y_copy(p, me.y).wait_send())
    me.others("y", lambda p: ay_copy(p, me.y).wait_send())
    me.others("yc", lambda p: b1_copy(p, me.yc).wait_send())
    me.others("z", lambda p: z_copy(p, me.z).wait_send())
    me.others("z", lambda p: az_copy(p, me.z).wait_send())
    me.others("z", lambda p: b2_copy(p, me.z).wait_send())


def reduce(rel_sum, ent_sum, plan):
    dma = pltpu.SemaphoreType.DMA
    block = pltpu.VMEM((NX, D, QUART), BF16)
    yblock = pltpu.VMEM((NY, YPAD, QUART), BF16)
    tile = pltpu.VMEM((NZ, 16, 128), BF16)
    b1 = pltpu.VMEM((NYC, 2 * NZ, D), BF16)
    b2 = pltpu.VMEM((NZ, 2 * NYC, D), BF16)
    sems = []
    for size in (NX, NX, NY, NZ, NZ, NY, NX, NX, NX, NYC, NZ):
        sems += [dma((size,)), dma((size,))]
    return pl.pallas_call(
        reduce_kernel,
        out_shape=(
            jax.ShapeDtypeStruct((D, NDOM), BF16),
            jax.ShapeDtypeStruct((D, RELS), BF16),
        ),
        in_specs=[VMEM] * 3,
        out_specs=(VMEM, VMEM),
        scratch_shapes=[block, block, block, yblock, yblock, tile, tile, tile, yblock, block, block, block]
        + [b1, b1, b2, b2]
        + sems,
        compiler_params=pltpu.CompilerParams(
            collective_id=1, has_side_effects=True, vmem_limit_bytes=40 << 20
        ),
        name="reduce_rows",
    )(rel_sum, ent_sum, plan)


def per_device(entity, relation, head_ids, relation_ids, tail_ids, negative_ids, span_counts, plan):
    plan_t = plan.T
    got = gather(jnp.transpose(entity, (1, 2, 0)), plan_t)
    rel_sum, ent_sum = span(
        got,
        relation.T,
        head_ids.reshape(1, SPAN),
        relation_ids.reshape(1, SPAN),
        tail_ids.reshape(1, SPAN),
        negative_ids,
        span_counts,
    )
    ent_out, rel_out = reduce(rel_sum, ent_sum, plan_t)
    return jnp.transpose(ent_out.reshape(1, D, NDOM), (2, 0, 1)), rel_out.T


def solution(mesh):
    placed = (
        P(None, "dom", None),
        P(),
        P(("dom", "rep")),
        P(("dom", "rep")),
        P(("dom", "rep")),
        P(("dom", "rep"), None),
        P(("dom", "rep")),
        P(),
    )
    return jax.shard_map(
        per_device,
        mesh=mesh,
        in_specs=placed,
        out_specs=(P(None, ("dom", "rep"), None), P()),
        check_vma=False,
    )
```

time: 466 us -> 136 us (0.29); the launches traced: 460 us -> 136 us
  blocking collectives: 184 us -> 0 us
  Pallas kernels: 0 us -> 128 us
  waiting for transfers between devices: 110 us -> 0 us
  other arithmetic: 46.7 us -> 0 us
  starting transfers between devices: 44.8 us -> 0 us
  local copies, waits for them, and re-layouts: 50.4 us -> 6.23 us
  between operations: 15.5 us -> 1.33 us
  matrix products: 8.87 us -> 0 us
    psum x1 -> x0, blocking collectives: 184 us -> none  [per_device(): relation_total = lax.psum(relation_sum, ('dom', 'rep'))]
    pallas_call x0 -> x3, Pallas kernels: none -> 128 us  [the longest x1 63.6 us: reduce(): pl.pallas_call(reduce_kernel, out_shape=(jax.ShapeDtypeStruct((D, NDOM),...]
    all_to_all x4 -> x0, waiting for transfers between devices: 110 us -> none  [the longest x1 40.9 us: per_device(): lax.all_to_all(tail_three, 'dom', split_axis=0, concat_axis=0, tiled=True)]
    all_to_all x4 -> x0, starting transfers between devices: 44.8 us -> none  [the longest x1 20.6 us: per_device(): lax.all_to_all(send_head, 'dom', split_axis=0, concat_axis=0, tiled=True)]
    scatter-add x4 -> x0, other arithmetic: 33.3 us -> none  [the longest x1 9.37 us: per_device(): jax.ops.segment_sum(relation_grad, relation_ids, num_segments=rel_count)]
    gather x9 -> x0, local copies, waits for them, and re-layouts: 25.5 us -> none  [the longest x2 7.4 us: per_device(): tail_block[tail_ids]]
    dot_general x5 -> x0, matrix products: 8.87 us -> none  [the longest x1 4.72 us: edge_grads(): lax.dot_general(negative_grad, queries_low, (((0,), (0,)), ((), ())), pre...]
    reshape x4 -> x0, local copies, waits for them, and re-layouts: 6.9 us -> none  [the longest x1 2.67 us: per_device(): head_three = head_sum.reshape(part_count, stripe, full_width)]
  transfers between devices with their start and end apart: 5 -> 0, of which waited for: 4 -> 0; matrix products, arithmetic and copies ran while one was open for 14% -> 0% of each run, Pallas kernels for 0% -> 0%
where the time goes in v1:
time: 136 us
  Pallas kernels  128 us (94%)
  local copies, waits for them, and re-layouts  6.23 us (5%)
    pallas_call x1, Pallas kernels, reduce(): pl.pallas_call(reduce_kernel, out_shape=(jax.ShapeDtypeStruct((D, NDOM),...  63.6 us
    pallas_call x1, Pallas kernels, gather(): pl.pallas_call(gather_kernel, out_shape=jax.ShapeDtypeStruct((NX, D, 2 *...  48.8 us
    pallas_call x1, Pallas kernels, span(): pl.pallas_call(span_kernel, out_shape=(jax.ShapeDtypeStruct((NC * NX, D,...  15.6 us
    unnamed x16, local copies, waits for them, and re-layouts  6.23 us

profile of v1, /device:TPU:1, one launch (start us, length us, event | category | flops | bytes accessed | tf_op | source)
XLA Modules:
  0.0 135.6 jit_solution(9049222625585399733)
XLA Ops:
  1.3 0.0 copy-start
  1.3 1.0 copy-done
  2.3 0.0 copy-start.5
  2.3 0.7 copy-done.5
  3.0 0.0 copy-start.6
  3.0 48.8 %gather_rows.1.got = bf16[4,400,256]{2,1,0:T(8,128)(2,1)S(1)} custom-call(bf16[4,400,128]{2,1,0:T(8,128)(2,1)S(1)} %bitcast.11, s32[2,128]{1,0:T(2,128)S(1)} %bitcast.16), custom_call_target="tpu_custom_call" | custom-call | tf_op jit(solution)/shard_map/gather_rows/pallas_call | solution.py:154
  51.8 0.0 copy-start.1
  51.8 0.7 copy-done.1
  52.5 0.0 copy-start.2
  52.5 0.7 copy-done.2
  53.2 0.0 copy-start.3
  53.2 0.7 copy-done.3
  53.8 0.0 copy-start.4
  53.8 0.7 copy-done.4
  54.5 15.6 %span_gradients.1 = (bf16[8,400,256]{2,1,0:T(8,128)(2,1)S(1)}, bf16[4,400,256]{2,1,0:T(8,128)(2,1)S(1)}) custom-call(bf16[4,400,256]{2,1,0:T(8,128)(2,1)S(1)} %gather_rows.1.got, bf16[400,2000]{1,0:T(8,128)(2,1)} %bitcast.18, s32[1,1000]{1,0:T(1,128)S(1)} %bitcast.13, s32[1,1000]{1,0:T(1,128)S(1)} %bitcast.14, s32[1,1000]{1,0:T(1,128)S(1)} %bitcast.15, ...), custom_call_target="tpu_custom_call" | custom-call | tf_op jit(solution)/shard_map/span_gradients/pallas_call | solution.py:251
  70.2 0.0 copy-done.6
  70.2 63.6 %reduce_rows.1 = (bf16[400,128]{1,0:T(8,128)(2,1)S(1)}, bf16[400,2000]{1,0:T(8,128)(2,1)S(1)}) custom-call(bf16[8,400,256]{2,1,0:T(8,128)(2,1)S(1)} %get-tuple-element.6.rel_sum, bf16[4,400,256]{2,1,0:T(8,128)(2,1)S(1)} %get-tuple-element.7.ent_sum, s32[2,128]{1,0:T(2,128)S(1)} %bitcast.17), custom_call_target="tpu_custom_call" | custom-call | tf_op jit(solution)/shard_map/reduce_rows/pallas_call | solution.py:451
  133.8 0.6 copy.13
  134.4 1.2 copy.14
Async XLA Ops:
  1.3 1.0 copy-start
  2.3 0.7 copy-start.5
  3.0 67.2 %copy-start.6 = (s32[128,2]{0,1:T(2,128)S(1)}, s32[128,2]{0,1:T(2,128)}, u32[]{:S(2)}) copy-start(s32[128,2]{0,1:T(2,128)} %param.15) | copy-start | bytes 3076
  51.8 0.7 copy-start.1
  52.5 0.7 copy-start.2
  53.2 0.7 copy-start.3
  53.8 0.7 copy-start.4

commit v2 on v0

v2 whole, which is shorter than its diff:
```python
import jax
import jax.numpy as jnp
from jax import lax
from jax.experimental import pallas as pl
from jax.experimental.pallas import tpu as pltpu
from jax.sharding import PartitionSpec as P

MESH = pl.DeviceIdType.MESH
F32, BF16, I32 = jnp.float32, jnp.bfloat16, jnp.int32
VMEM = pl.BlockSpec(memory_space=pltpu.VMEM)
HBM = pl.BlockSpec(memory_space=pltpu.HBM)

NY, NZ, NC, NX = 4, 16, 2, 4
NYC = NY * NC
NDOM = NY * NZ * NC
D = 400
HALF = D // 2
RELS = 2000
RELPAD = 2048
SPAN = 1000
SLOTS = 1024
CHUNK = 256
ROWS = 512
WIDE = 256
PIECES = ((0, 128), (128, 128), (256, 128), (384, 16))
NP = len(PIECES)
NH = 2
LANES = 128
XROWS = 112
XTILES = XROWS // 16
NEVER = -1e30


def nn(a, b):
    return lax.dot_general(a, b, (((1,), (0,)), ((), ())), preferred_element_type=F32)


def nt(a, b):
    return lax.dot_general(a, b, (((1,), (1,)), ((), ())), preferred_element_type=F32)


def tn(a, b):
    return lax.dot_general(a, b, (((0,), (0,)), ((), ())), preferred_element_type=F32)


def iota(shape, axis):
    return lax.broadcasted_iota(I32, shape, axis)


def onehot(hit):
    return jnp.where(hit, 1.0, 0.0).astype(BF16)


class Place:
    def __init__(self):
        dom, self.x = lax.axis_index("dom"), lax.axis_index("rep")
        self.c = lax.rem(dom, NC)
        self.z = lax.rem(lax.div(dom, NC), NZ)
        self.y = lax.div(dom, NC * NZ)
        self.yc = self.y * NC + self.c

    def at(self, z=None, y=None, yc=None, x=None):
        z = self.z if z is None else z
        x = self.x if x is None else x
        if y is not None:
            yc = y * NC + self.c
        yc = self.yc if yc is None else yc
        return {"dom": (lax.div(yc, NC) * NZ + z) * NC + lax.rem(yc, NC), "rep": x}

    def others(self, axis, body):
        size, me = {"z": (NZ, self.z), "yc": (NYC, self.yc), "x": (NX, self.x), "y": (NY, self.y)}[axis]

        def step(k, carry):
            body(lax.rem(me + k, size))
            return carry

        lax.fori_loop(1, size, step, 0)

    def greet(self, sem):
        def hello(**where):
            pl.semaphore_signal(sem, inc=1, device_id=self.at(**where), device_id_type=MESH)

        self.others("z", lambda p: hello(z=p))
        self.others("yc", lambda p: hello(yc=p))
        self.others("x", lambda p: hello(x=p))


def remote(src, dst, send, recv, where):
    return pltpu.make_async_remote_copy(
        src_ref=src, dst_ref=dst, send_sem=send, recv_sem=recv, device_id=where, device_id_type=MESH
    )


def arrived(group, sem):
    pltpu.make_async_copy(group, group, sem).wait()


SQUARE = (2 * NDOM, 2 * NDOM)


def bits(v, low, count):
    return lax.bitwise_and(lax.shift_right_logical(v, low), (1 << count) - 1)


def by_send_order():
    row, col = iota(SQUARE, 0), iota(SQUARE, 1)
    worker = (bits(row, 2, 2) * NZ + bits(row, 4, 4)) * NC + bits(row, 1, 1)
    return onehot(col == bits(row, 0, 1) * NDOM + worker)


def swap_zy():
    row, col = iota(SQUARE, 0), iota(SQUARE, 1)
    return onehot(col == bits(row, 1, 4) * 16 + bits(row, 5, 3) * 2 + bits(row, 0, 1))


def by_owner():
    row, col = iota(SQUARE, 0), iota(SQUARE, 1)
    owner = (bits(row, 6, 2) * NZ + bits(row, 1, 4)) * NC + bits(row, 5, 1)
    return onehot(col == bits(row, 0, 1) * NDOM + owner)


def kernel(
    count, ent_hbm, rel_hbm, head_hbm, relid_hbm, tail_hbm, neg_hbm, plan_hbm,
    ent_out, rel_out,
    stripe, rel, plan, raw, ids,
    snd1, rcv1, snd2, rcv2, gx,
    hb, tb, tr, logc, h1, t1, r1, ht, rt, tt, dr, dh, av, ql,
    es, rex, sb1, rb1, sb2, rb2,
    oc, rc, ys, ry, xs, rx, zs, rz, agz, agx, agxy, agxc, agyx, agyc,
    s_in, s_1, r_1, s_2, r_2, s_3, r_3,
    s_e, r_e, s_b1, r_b1, s_b2, r_b2,
    s_c, r_c, s_y, r_y, s_x, r_x, s_z, r_z, s_az, r_az,
    s_ax, r_ax, s_axy, r_axy, s_axc, r_axc, s_ay, r_ay, s_ayx, r_ayx, s_ayc, r_ayc,
):
    me = Place()
    loads = [
        pltpu.make_async_copy(plan_hbm, plan, s_in.at[0]),
        pltpu.make_async_copy(ent_hbm.at[me.x], stripe, s_in.at[1]),
        pltpu.make_async_copy(head_hbm, raw.at[0], s_in.at[2]),
        pltpu.make_async_copy(relid_hbm, raw.at[1], s_in.at[3]),
        pltpu.make_async_copy(tail_hbm, raw.at[2], s_in.at[4]),
        pltpu.make_async_copy(neg_hbm, raw.at[3], s_in.at[5]),
        pltpu.make_async_copy(rel_hbm, rel, s_in.at[6]),
    ]
    for load in loads:
        load.start()
    hello = pltpu.get_barrier_semaphore()
    me.greet(hello)

    loads[0].wait()
    loads[1].wait()
    sq = (NDOM, NDOM)
    plan_hit = jnp.concatenate([onehot(iota(sq, 0) == plan[h : h + 1, :]) for h in range(2)], axis=1)
    picked = nn(stripe[...], plan_hit).astype(BF16)
    rows = nt(by_send_order(), picked).astype(BF16)
    for p, (d, n) in enumerate(PIECES):
        snd1[p, :, :, 0:n] = rows[:, d : d + n].reshape(NZ, 2 * NYC, n)
        if n < LANES:
            snd1[p, :, :, n:] = jnp.zeros((NZ, 2 * NYC, LANES - n), BF16)

    def copy1(p, dst, src):
        return remote(snd1.at[p, dst], rcv1.at[p, src], s_1, r_1.at[p], me.at(z=dst))

    def copy2(p, dst, src):
        return remote(snd2.at[p, dst], rcv2.at[p, src], s_2, r_2.at[p], me.at(yc=dst))

    def copy3(p, dst, src):
        part = gx.at[src, pl.ds(*PIECES[p])]
        return remote(part, part, s_3, r_3.at[p], me.at(x=dst))
    pl.semaphore_wait(hello, NX + NYC + NZ - 3)
    for p in range(NP):
        me.others("z", lambda q, p=p: copy1(p, q, me.z).start())
        rcv1[p, me.z] = snd1[p, me.z]

    def over_yc(p):
        arrived(rcv1.at[p, pl.ds(0, NZ - 1)], r_1.at[p])
        turned = nn(swap_zy(), rcv1[p].reshape(2 * NDOM, LANES)).astype(BF16)
        snd2[p] = turned.reshape(NYC, 2 * NZ, LANES)
        me.others("yc", lambda q: copy2(p, q, me.yc).start())
        rcv2[p, me.yc] = snd2[p, me.yc]

    def over_x(p):
        d, n = PIECES[p]
        arrived(rcv2.at[p, pl.ds(0, NYC - 1)], r_2.at[p])
        turned = tn(rcv2[p].reshape(2 * NDOM, LANES), by_owner()).astype(BF16)
        gx[me.x, d : d + n] = turned[0:n]
        me.others("x", lambda q: copy3(p, q, me.x).start())

    def relation_rows(k):
        at = slice(k * CHUNK, (k + 1) * CHUNK)
        r1[:, at] = onehot(iota((RELPAD, CHUNK), 0) == ids[1:2, at])
        rt[:, at] = nn(rel[...], r1[0:RELS, at]).astype(BF16)
    for load in loads[2:6]:
        load.wait()
    ids[...] = jnp.full(ids.shape, -4, I32)
    for k in range(4):
        ids[k : k + 1, 0:SPAN] = raw[k]
    given = ids[...]
    place = lax.bitwise_and(given, 3) * NDOM + lax.shift_right_arithmetic(given, 2)
    ids[...] = jnp.where(iota(ids.shape, 0) == 1, given, place)
    loads[6].wait()
    relation_rows(0)
    relation_rows(1)
    over_yc(0)
    relation_rows(2)
    over_yc(1)
    over_x(0)
    relation_rows(3)
    over_yc(2)
    over_x(1)
    times = jnp.zeros((ROWS, 1), F32)
    for k in range(SLOTS // CHUNK):
        at = slice(k * CHUNK, (k + 1) * CHUNK)
        hit = iota((ROWS, CHUNK), 0) == ids[3:4, at]
        times += jnp.sum(jnp.where(hit, 1.0, 0.0), axis=1, keepdims=True)
        h1[:, at] = onehot(iota((ROWS, CHUNK), 0) == ids[0:1, at])
        t1[:, at] = onehot(iota((ROWS, CHUNK), 0) == ids[2:3, at])
    logc[...] = jnp.where(times > 0.0, jnp.log(jnp.maximum(times, 1.0)), NEVER)
    over_yc(3)
    over_x(2)
    over_x(3)
    for p, (d, n) in enumerate(PIECES):
        arrived(gx.at[pl.ds(0, NX - 1), pl.ds(d, n)], r_3.at[p])
        for x in range(NX):
            lanes = slice(x * NDOM, (x + 1) * NDOM)
            hb[d : d + n, lanes] = gx[x, d : d + n, 0:NDOM]
            tb[d : d + n, lanes] = gx[x, d : d + n, NDOM:]
        tr[:, d : d + n] = tb[d : d + n, :].T
        ht[d : d + n, :] = nn(hb[d : d + n, :], h1[...]).astype(BF16)
        tt[d : d + n, :] = nn(tb[d : d + n, :], t1[...]).astype(BF16)

    def chunk(k, carry):
        at = pl.ds(pl.multiple_of(k * CHUNK, CHUNK), CHUNK)
        h, r, t = ht[:, at].astype(F32), rt[:, at].astype(F32), tt[:, at].astype(F32)
        h_re, h_im = h[0:HALF], h[HALF:D]
        r_re, r_im = r[0:HALF], r[HALF:D]
        q_re = h_re * r_re - h_im * r_im
        q_im = h_re * r_im + h_im * r_re
        s0 = jnp.sum(q_re * t[0:HALF] + q_im * t[HALF:D], axis=0, keepdims=True)
        q_low = jnp.concatenate([q_re, q_im], axis=0).astype(BF16)
        ql[:, at] = q_low
        s = nn(tr[...], q_low) + logc[...]
        m = jnp.maximum(s0, jnp.max(s, axis=0, keepdims=True))
        e0 = jnp.exp(s0 - m)
        e = jnp.exp(s - m)
        z = e0 + jnp.sum(e, axis=0, keepdims=True)
        slot = iota((1, CHUNK), 1) + k * CHUNK
        valid = jnp.where(slot < count[0], 1.0, 0.0)
        g0 = valid * (e0 / z - 1.0)
        tail_hit = iota((ROWS, CHUNK), 0) == ids[2:3, at]
        a = (e * (valid / z) + jnp.where(tail_hit, g0, 0.0)).astype(BF16)
        av[:, at] = a
        dq = nn(tb[...], a)
        d_re, d_im = dq[0:HALF], dq[HALF:D]
        dh[:, at] = jnp.concatenate(
            [d_re * r_re + d_im * r_im, d_im * r_re - d_re * r_im], axis=0
        ).astype(BF16)
        dr[:, at] = jnp.concatenate(
            [d_re * h_re + d_im * h_im, d_im * h_re - d_re * h_im], axis=0
        ).astype(BF16)
        return carry
    lax.fori_loop(0, SLOTS // CHUNK, chunk, 0)

    def ent_copy(p, dst, src):
        part = pl.ds(*PIECES[p])
        return remote(es.at[dst, part], rex.at[src, part], s_e, r_e.at[p], me.at(x=dst))

    def b1_copy(p, dst, src):
        return remote(sb1.at[p, dst], rb1.at[p, src], s_b1, r_b1.at[p], me.at(yc=dst))

    def b2_copy(p, dst, src):
        return remote(sb2.at[p, dst], rb2.at[p, src], s_b2, r_b2.at[p], me.at(z=dst))

    other_core = me.at(yc=me.y * NC + (1 - me.c))

    def core_copy(y):
        return remote(oc.at[y], rc.at[y], s_c, r_c.at[y], other_core)

    def y_copy(dst, src):
        return remote(ys.at[dst], ry.at[src], s_y, r_y, me.at(y=dst))

    def x_copy(dst, src):
        return remote(xs.at[dst], rx.at[src], s_x, r_x, me.at(x=dst))

    def z_copy(dst, src):
        return remote(zs.at[dst], rz.at[src], s_z.at[dst], r_z, me.at(z=dst))

    def az_copy(dst, src):
        return remote(agz.at[src], agz.at[src], s_az, r_az.at[src], me.at(z=dst))

    def ax_copy(dst, src):
        return remote(agx.at[src], agx.at[src], s_ax, r_ax, me.at(x=dst))

    def axy_copy(dst, src):
        return remote(agxy.at[src], agxy.at[src], s_axy, r_axy.at[src], me.at(y=dst))

    def axc_copy(y):
        return remote(agxy.at[y], agxc.at[y], s_axc, r_axc, other_core)

    def ay_copy(dst, src):
        part = agyx.at[me.x, src]
        return remote(part, part, s_ay, r_ay, me.at(y=dst))

    def ayx_copy(dst, src):
        return remote(agyx.at[src], agyx.at[src], s_ayx, r_ayx.at[src], me.at(x=dst))

    def ayc_copy(x):
        return remote(agyx.at[x], agyc.at[x], s_ayc, r_ayc, other_core)

    def entity_block(x):
        lanes = pl.ds(pl.multiple_of(x * NDOM, NDOM), NDOM)
        es[x, :, 0:NDOM] = nt(dh[...], h1[lanes, :]).astype(BF16)
        es[x, :, NDOM : 2 * NDOM] = nt(ql[...], av[lanes, :]).astype(BF16)

    def entity_block_out(x):
        entity_block(x)
        for p in range(NP):
            ent_copy(p, x, me.x).start()

    def relation_block(c, y):
        lanes = pl.ds(pl.multiple_of((c * NY + y) * WIDE, WIDE), WIDE)
        return nt(dr[...], r1[lanes, :])

    def to_core(y):
        oc[y] = relation_block(1 - me.c, y).astype(BF16)
        core_copy(y).start()

    def with_core(y):
        block = relation_block(me.c, y)
        core_copy(y).wait_recv()
        ys[y] = (block + rc[y].astype(F32)).astype(BF16)

    def with_core_out(y):
        with_core(y)
        y_copy(y, me.y).start()

    def four(ref):
        return ref[0].astype(F32) + ref[1].astype(F32) + ref[2].astype(F32) + ref[3].astype(F32)

    def rel_x():
        ry[me.y] = ys[me.y]
        arrived(ry.at[pl.ds(0, NY - 1)], r_y)
        total = four(ry).astype(BF16)
        for x in range(NX):
            n = min(XROWS, D - x * XROWS)
            xs[x, 0:n] = total[x * XROWS : x * XROWS + n]
            if n < XROWS:
                xs[x, n:] = jnp.zeros((XROWS - n, WIDE), BF16)
        me.others("x", lambda q: x_copy(q, me.x).start())

    def tiles(body):
        def step(i, carry):
            z = lax.div(i, XTILES) * 8 + lax.rem(i, XTILES)

            @pl.when(z != me.z)
            def _():
                body(z)

            return carry

        lax.fori_loop(0, NH * XTILES, step, 0)

    def rel_z():
        rx[me.x] = xs[me.x]
        arrived(rx.at[pl.ds(0, NX - 1)], r_x)
        total = four(rx).astype(BF16)
        for h in range(NH):
            half = total[:, h * LANES : (h + 1) * LANES]
            zs[h * 8 : h * 8 + XTILES] = half.reshape(XTILES, 16, LANES)
        tiles(lambda q: z_copy(q, me.z).start())

    owns = lax.rem(me.z, 8) < XTILES

    def rel_az():
        @pl.when(owns)
        def _():
            rz[me.z] = zs[me.z]
            arrived(rz.at[pl.ds(0, NZ - 1)], r_z)
            total = rz[0].astype(F32)
            for z in range(1, NZ):
                total += rz[z].astype(F32)
            agz[me.z] = total.astype(BF16)
            me.others("z", lambda q: az_copy(q, me.z).start())

    def rel_back1():
        tiles(lambda q: az_copy(q, q).wait_recv())
        agx[me.x] = agz[0:XTILES].reshape(XROWS, LANES)
        me.others("x", lambda q: ax_copy(q, me.x).start())
        agyx[me.x, me.y] = agz[8 : 8 + XTILES].reshape(XROWS, LANES)
        me.others("y", lambda q: ay_copy(q, me.y).start())

    def rel_back2():
        arrived(agx.at[pl.ds(0, NX - 1)], r_ax)
        for x in range(NX):
            n = min(XROWS, D - x * XROWS)
            agxy[me.y, x * XROWS : x * XROWS + n] = agx[x, 0:n]
        me.others("y", lambda q: axy_copy(q, me.y).start())
        arrived(agyx.at[0, pl.ds(0, NY - 1)], r_ay)
        me.others("x", lambda q: ayx_copy(q, me.x).start())
        axc_copy(me.y).start()
        ayc_copy(me.x).start()

    def rel_core():
        def step(k, carry):
            y = lax.rem(me.y + k, NY)
            axy_copy(y, y).wait_recv()
            axc_copy(y).start()
            x = lax.rem(me.x + k, NX)
            ayx_copy(x, x).wait_recv()
            ayc_copy(x).start()
            return carry

        lax.fori_loop(1, NX, step, 0)

    def rel_place(c, sub, block, rows):
        start = (c * NY * NH + sub) * LANES
        n = min(LANES, RELS - start)
        rel_out[rows[0] : rows[1], start : start + n] = block.astype(BF16)[:, 0:n]

    def rel_done():
        arrived(agxc, r_axc)
        arrived(agyc, r_ayc)
        first = me.c == 0

        def both(here, there, sub, rows):
            here, there = here.astype(F32), there.astype(F32)
            rel_place(0, sub, jnp.where(first, here, there), rows)
            rel_place(1, sub, jnp.where(first, there, here), rows)

        for y in range(NY):
            both(agxy[y], agxc[y], y * NH, (0, D))
            for x in range(NX):
                n = min(XROWS, D - x * XROWS)
                both(agyx[x, y, 0:n], agyc[x, y, 0:n], y * NH + 1, (x * XROWS, x * XROWS + n))

    def ent_yc(p):
        d, n = PIECES[p]
        rex[me.x, d : d + n] = es[me.x, d : d + n]
        arrived(rex.at[pl.ds(0, NX - 1), pl.ds(d, n)], r_e.at[p])
        total = sum(rex[x, d : d + n].astype(F32) for x in range(NX)).astype(BF16)
        turned = nt(by_owner(), total).astype(BF16).reshape(NYC, 2 * NZ, n)
        sb1[p, :, :, 0:n] = turned
        if n < LANES:
            sb1[p, :, :, n:] = jnp.zeros((NYC, 2 * NZ, LANES - n), BF16)
        me.others("yc", lambda q: b1_copy(p, q, me.yc).start())
        rb1[p, me.yc] = sb1[p, me.yc]

    def ent_rows(p):
        arrived(rb1.at[p, pl.ds(0, NYC - 1)], r_b1.at[p])
        turned = tn(swap_zy(), rb1[p].reshape(2 * NDOM, LANES)).astype(BF16)
        sb2[p] = turned.reshape(NZ, 2 * NYC, LANES)
        rb2[p, me.z] = sb2[p, me.z]

    def ent_z(p):
        me.others("z", lambda q: b2_copy(p, q, me.z).start())

    def ent_done(p, pick):
        d, n = PIECES[p]
        arrived(rb2.at[p, pl.ds(0, NZ - 1)], r_b2.at[p])
        ent_out[d : d + n, :] = tn(rb2[p].reshape(2 * NDOM, LANES), pick)[0:n].astype(BF16)
    me.others("x", entity_block_out)
    entity_block(me.x)
    me.others("y", to_core)
    to_core(me.y)
    me.others("y", with_core_out)
    with_core(me.y)
    for p in range(NP):
        ent_yc(p)
    for p in range(NP):
        ent_rows(p)
    ent_z(0)
    rel_x()
    rel_z()
    parts = jnp.concatenate([onehot(iota(sq, 0) == plan[h : h + 1, :]) for h in range(2)], axis=1)
    pick = nt(by_send_order(), parts).astype(BF16)
    rel_az()
    rel_back1()
    for p in range(1, NP):
        ent_z(p)
    rel_back2()
    rel_core()
    for p in range(NP):
        ent_done(p, pick)
    rel_done()
    arrived(snd1.at[:, pl.ds(0, NZ - 1)], s_1)
    arrived(snd2.at[:, pl.ds(0, NYC - 1)], s_2)
    arrived(gx.at[pl.ds(0, NX - 1)], s_3)
    arrived(es.at[pl.ds(0, NX - 1)], s_e)
    arrived(sb1.at[:, pl.ds(0, NYC - 1)], s_b1)
    arrived(sb2.at[:, pl.ds(0, NZ - 1)], s_b2)
    arrived(oc, s_c)
    arrived(ys.at[pl.ds(0, NY - 1)], s_y)
    arrived(xs.at[pl.ds(0, NX - 1)], s_x)
    arrived(agx.at[pl.ds(0, NX - 1)], s_ax)
    arrived(agyx.at[0, pl.ds(0, NY - 1)], s_ay)
    arrived(agxy.at[pl.ds(0, NY - 1)], s_axy)
    arrived(agyx.at[pl.ds(0, NX - 1)], s_ayx)
    arrived(agxc, s_axc)
    arrived(agyc, s_ayc)
    tiles(lambda q: z_copy(q, me.z).wait_send())

    @pl.when(owns)
    def _():
        arrived(agz.at[pl.ds(0, NZ - 1)], s_az)


def scratch():
    def bf16(*shape):
        return pltpu.VMEM(shape, BF16)

    dma = pltpu.SemaphoreType.DMA

    by_z, by_yc = bf16(NP, NZ, 2 * NYC, LANES), bf16(NP, NYC, 2 * NZ, LANES)
    block, slots, half = bf16(NX, D, WIDE), bf16(D, SLOTS), bf16(NY, D, LANES)
    small, tile = bf16(NX, XROWS, WIDE), bf16(NZ, 16, LANES)
    thin, quads = bf16(NX, XROWS, LANES), bf16(NX, NY, XROWS, LANES)
    return (
        [bf16(D, NDOM), bf16(D, RELS), pltpu.VMEM((2, NDOM), I32)]
        + [pltpu.VMEM((4, 1, SPAN), I32), pltpu.VMEM((8, SLOTS), I32)]
        + [by_z, by_z, by_yc, by_yc, block]
        + [bf16(D, ROWS), bf16(D, ROWS), bf16(ROWS, D), pltpu.VMEM((ROWS, 1), F32)]
        + [bf16(ROWS, SLOTS), bf16(ROWS, SLOTS), bf16(RELPAD, SLOTS)]
        + [slots, slots, slots, slots, slots, bf16(ROWS, SLOTS), slots]
        + [block, block, by_yc, by_yc, by_z, by_z]
        + [block, block, block, block, small, small, tile, tile, tile]
        + [thin, half, half, quads, quads]
        + [dma((7,))]
        + [dma, dma((NP,))] * 6
        + [dma, dma((NY,)), dma, dma, dma, dma, dma((NZ,)), dma, dma, dma((NZ,))]
        + [dma, dma, dma, dma((NY,)), dma, dma]
        + [dma, dma, dma, dma((NX,)), dma, dma]
    )


def per_device(entity, relation, head_ids, relation_ids, tail_ids, negative_ids, span_counts, plan):
    ent_out, rel_out = pl.pallas_call(
        kernel,
        out_shape=(
            jax.ShapeDtypeStruct((D, NDOM), BF16),
            jax.ShapeDtypeStruct((D, RELS), BF16),
        ),
        in_specs=[pl.BlockSpec(memory_space=pltpu.SMEM)] + [HBM] * 7,
        out_specs=(VMEM, VMEM),
        scratch_shapes=scratch(),
        compiler_params=pltpu.CompilerParams(
            collective_id=0, has_side_effects=True, vmem_limit_bytes=40 << 20
        ),
        name="bucket_round",
    )(
        span_counts,
        *(
            pltpu.with_memory_space_constraint(v, pltpu.HBM)
            for v in (
                jnp.transpose(entity, (1, 2, 0)),
                relation.T,
                head_ids.reshape(1, SPAN),
                relation_ids.reshape(1, SPAN),
                tail_ids.reshape(1, SPAN),
                negative_ids,
                plan.T,
            )
        ),
    )
    return jnp.transpose(ent_out.reshape(1, D, NDOM), (2, 0, 1)), rel_out.T


def solution(mesh):
    placed = (
        P(None, "dom", None),
        P(),
        P(("dom", "rep")),
        P(("dom", "rep")),
        P(("dom", "rep")),
        P(("dom", "rep"), None),
        P(("dom", "rep")),
        P(),
    )
    return jax.shard_map(
        per_device,
        mesh=mesh,
        in_specs=placed,
        out_specs=(P(None, ("dom", "rep"), None), P()),
        check_vma=False,
    )
```

time: 466 us -> 103 us (0.22); the launches traced: 460 us -> 103 us
  blocking collectives: 184 us -> 0 us
  waiting for transfers between devices: 110 us -> 0 us
  Pallas kernels: 0 us -> 99.8 us
  local copies, waits for them, and re-layouts: 50.4 us -> 1.81 us
  other arithmetic: 46.7 us -> 0 us
  starting transfers between devices: 44.8 us -> 0 us
  between operations: 15.5 us -> 1.29 us
  matrix products: 8.87 us -> 0 us
    psum x1 -> x0, blocking collectives: 184 us -> none  [per_device(): relation_total = lax.psum(relation_sum, ('dom', 'rep'))]
    all_to_all x4 -> x0, waiting for transfers between devices: 110 us -> none  [the longest x1 40.9 us: per_device(): lax.all_to_all(tail_three, 'dom', split_axis=0, concat_axis=0, tiled=True)]
    pallas_call x0 -> x1, Pallas kernels: none -> 99.8 us  [per_device(): pl.pallas_call(kernel, out_shape=(jax.ShapeDtypeStruct((D, NDOM), BF16),...]
    all_to_all x4 -> x0, starting transfers between devices: 44.8 us -> none  [the longest x1 20.6 us: per_device(): lax.all_to_all(send_head, 'dom', split_axis=0, concat_axis=0, tiled=True)]
    scatter-add x4 -> x0, other arithmetic: 33.3 us -> none  [the longest x1 9.37 us: per_device(): jax.ops.segment_sum(relation_grad, relation_ids, num_segments=rel_count)]
    gather x9 -> x0, local copies, waits for them, and re-layouts: 25.5 us -> none  [the longest x2 7.4 us: per_device(): tail_block[tail_ids]]
    dot_general x5 -> x0, matrix products: 8.87 us -> none  [the longest x1 4.72 us: edge_grads(): lax.dot_general(negative_grad, queries_low, (((0,), (0,)), ((), ())), pre...]
    unnamed x33 -> x2, local copies, waits for them, and re-layouts: 9.34 us -> 1.81 us
  transfers between devices with their start and end apart: 5 -> 0, of which waited for: 4 -> 0; matrix products, arithmetic and copies ran while one was open for 14% -> 0% of each run, Pallas kernels for 0% -> 0%
where the time goes in v2:
time: 103 us
  Pallas kernels  99.8 us (97%)
  local copies, waits for them, and re-layouts  1.81 us (2%)
  between operations  1.29 us (1%)
    pallas_call x1, Pallas kernels, per_device(): pl.pallas_call(kernel, out_shape=(jax.ShapeDtypeStruct((D, NDOM), BF16),...  99.8 us

profile of v2, /device:TPU:1, one launch (start us, length us, event | category | flops | bytes accessed | tf_op | source)
XLA Modules:
  0.0 102.9 jit_solution(8042363121104434129)
XLA Ops:
  1.3 99.8 %bucket_round.1 = (bf16[400,128]{1,0:T(8,128)(2,1)S(1)}, bf16[400,2000]{1,0:T(8,128)(2,1)S(1)}) custom-call(s32[1]{0:T(128)S(6)} %copy.12.count, bf16[4,400,128]{2,1,0:T(8,128)(2,1)} %bitcast.13, bf16[400,2000]{1,0:T(8,128)(2,1)} %bitcast.12, s32[1,1000]{1,0:T(1,128)} %bitcast.14, s32[1,1000]{1,0:T(1,128)} %bitcast.15, s32[1,1000]{1,0:T(1,128)} %bitcast.16, ...), custom_call_target="tpu_custom_call" | custom-call | tf_op jit(solution)/shard_map/bucket_round/pallas_call | solution.py:536
  101.1 0.6 copy.13
  101.8 1.2 %copy.14 = bf16[2000,400]{0,1:T(8,128)(2,1)} copy(bf16[2000,400]{0,1:T(8,128)(2,1)S(1)} %bitcast.10) | data formatting | bytes 3200000

commit v3 on v2

v3 whole, which is shorter than its diff:
```python
import jax
import jax.numpy as jnp
from jax import lax
from jax.experimental import pallas as pl
from jax.experimental.pallas import tpu as pltpu
from jax.sharding import PartitionSpec as P

MESH = pl.DeviceIdType.MESH
F32, BF16, I32 = jnp.float32, jnp.bfloat16, jnp.int32
VMEM = pl.BlockSpec(memory_space=pltpu.VMEM)
HBM = pl.BlockSpec(memory_space=pltpu.HBM)

NY, NZ, NC, NX = 4, 16, 2, 4
NYC = NY * NC
NDOM = NY * NZ * NC
D = 400
HALF = D // 2
RELS = 2000
RELPAD = 2048
SPAN = 1000
SLOTS = 1024
CHUNK = 256
ROWS = 512
WIDE = 256
PIECES = ((0, 256), (256, 128), (384, 16))
NP = len(PIECES)
BACK = ((0, 256), (256, 144))
NB = len(BACK)
NH = 2
LANES = 128
XROWS = 112
XTILES = XROWS // 16
NEVER = -1e30


def nn(a, b):
    return lax.dot_general(a, b, (((1,), (0,)), ((), ())), preferred_element_type=F32)


def nt(a, b):
    return lax.dot_general(a, b, (((1,), (1,)), ((), ())), preferred_element_type=F32)


def tn(a, b):
    return lax.dot_general(a, b, (((0,), (0,)), ((), ())), preferred_element_type=F32)


def iota(shape, axis):
    return lax.broadcasted_iota(I32, shape, axis)


def onehot(hit):
    return jnp.where(hit, 1.0, 0.0).astype(BF16)


class Place:
    def __init__(self):
        dom, self.x = lax.axis_index("dom"), lax.axis_index("rep")
        self.c = lax.rem(dom, NC)
        self.z = lax.rem(lax.div(dom, NC), NZ)
        self.y = lax.div(dom, NC * NZ)
        self.yc = self.y * NC + self.c

    def at(self, z=None, y=None, yc=None, x=None):
        z = self.z if z is None else z
        x = self.x if x is None else x
        if y is not None:
            yc = y * NC + self.c
        yc = self.yc if yc is None else yc
        return {"dom": (lax.div(yc, NC) * NZ + z) * NC + lax.rem(yc, NC), "rep": x}

    def others(self, axis, body):
        size, me = {"z": (NZ, self.z), "yc": (NYC, self.yc), "x": (NX, self.x), "y": (NY, self.y)}[axis]

        def step(k, carry):
            away = size // 2 + lax.div(k, 2) * (1 - 2 * lax.rem(k, 2))
            body(lax.rem(me + away, size))
            return carry

        lax.fori_loop(1, size, step, 0)

    def greet(self, sem):
        def hello(**where):
            pl.semaphore_signal(sem, inc=1, device_id=self.at(**where), device_id_type=MESH)

        self.others("z", lambda p: hello(z=p))
        self.others("yc", lambda p: hello(yc=p))
        self.others("x", lambda p: hello(x=p))


def remote(src, dst, send, recv, where):
    return pltpu.make_async_remote_copy(
        src_ref=src, dst_ref=dst, send_sem=send, recv_sem=recv, device_id=where, device_id_type=MESH
    )


def arrived(group, sem):
    pltpu.make_async_copy(group, group, sem).wait()


SQUARE = (2 * NDOM, 2 * NDOM)


def bits(v, low, count):
    return lax.bitwise_and(lax.shift_right_logical(v, low), (1 << count) - 1)


def by_send_order():
    row, col = iota(SQUARE, 0), iota(SQUARE, 1)
    worker = (bits(row, 2, 2) * NZ + bits(row, 4, 4)) * NC + bits(row, 1, 1)
    return onehot(col == bits(row, 0, 1) * NDOM + worker)


def swap_zy():
    row, col = iota(SQUARE, 0), iota(SQUARE, 1)
    return onehot(col == bits(row, 1, 4) * 16 + bits(row, 5, 3) * 2 + bits(row, 0, 1))


def by_owner():
    row, col = iota(SQUARE, 0), iota(SQUARE, 1)
    owner = (bits(row, 6, 2) * NZ + bits(row, 1, 4)) * NC + bits(row, 5, 1)
    return onehot(col == bits(row, 0, 1) * NDOM + owner)


def kernel(
    count, ent_hbm, rel_hbm, head_hbm, relid_hbm, tail_hbm, neg_hbm, plan_hbm,
    ent_out, rel_out,
    stripe, rel, plan, raw, ids,
    snd1, rcv1, snd2, rcv2, gx,
    hb, tb, tr, logc, h1, t1, r1, ht, rt, tt, dr, dh, av, ql,
    es, rex, sb1, rb1, sb2, rb2,
    oc, rc, asend, aland, bsend, bland, zs, rz, agz, dback, fback, gback,
    s_in, s_1, r_1, s_2, r_2, s_3, r_3,
    s_e, r_e, s_b1, r_b1, s_b2, r_b2,
    s_c, r_c, s_a, r_a, s_b, r_b, s_z, r_z, s_az, r_az, s_d, r_d, s_f, r_f, s_g, r_g,
):
    me = Place()
    loads = [
        pltpu.make_async_copy(plan_hbm, plan, s_in.at[0]),
        pltpu.make_async_copy(ent_hbm.at[me.x], stripe, s_in.at[1]),
        pltpu.make_async_copy(head_hbm, raw.at[0], s_in.at[2]),
        pltpu.make_async_copy(relid_hbm, raw.at[1], s_in.at[3]),
        pltpu.make_async_copy(tail_hbm, raw.at[2], s_in.at[4]),
        pltpu.make_async_copy(neg_hbm, raw.at[3], s_in.at[5]),
        pltpu.make_async_copy(rel_hbm, rel, s_in.at[6]),
    ]
    for load in loads:
        load.start()
    hello = pltpu.get_barrier_semaphore()
    me.greet(hello)

    loads[0].wait()
    loads[1].wait()
    sq = (NDOM, NDOM)
    plan_hit = jnp.concatenate([onehot(iota(sq, 0) == plan[h : h + 1, :]) for h in range(2)], axis=1)
    picked = nn(stripe[...], plan_hit).astype(BF16)
    rows = nt(by_send_order(), picked).astype(BF16)
    for p, (d, n) in enumerate(PIECES):
        snd1[p][...] = rows[:, d : d + n].reshape(NZ, 2 * NYC, n)

    def copy1(p, dst, src):
        return remote(snd1[p].at[dst], rcv1[p].at[src], s_1.at[p], r_1.at[p], me.at(z=dst))

    def copy2(p, dst, src):
        return remote(snd2[p].at[dst], rcv2[p].at[src], s_2.at[p], r_2.at[p], me.at(yc=dst))

    def copy3(p, dst, src):
        part = gx.at[src, pl.ds(*PIECES[p])]
        return remote(part, part, s_3, r_3.at[p], me.at(x=dst))
    pl.semaphore_wait(hello, NX + NYC + NZ - 3)
    for p in range(NP):
        me.others("z", lambda q, p=p: copy1(p, q, me.z).start())
        rcv1[p][me.z] = snd1[p][me.z]

    def over_yc(p):
        arrived(rcv1[p].at[pl.ds(0, NZ - 1)], r_1.at[p])
        turned = nn(swap_zy(), rcv1[p][...].reshape(2 * NDOM, PIECES[p][1])).astype(BF16)
        snd2[p][...] = turned.reshape(NYC, 2 * NZ, PIECES[p][1])
        me.others("yc", lambda q: copy2(p, q, me.yc).start())
        rcv2[p][me.yc] = snd2[p][me.yc]

    def over_x(p):
        d, n = PIECES[p]
        arrived(rcv2[p].at[pl.ds(0, NYC - 1)], r_2.at[p])
        turned = tn(rcv2[p][...].reshape(2 * NDOM, n), by_owner()).astype(BF16)
        gx[me.x, d : d + n] = turned
        me.others("x", lambda q: copy3(p, q, me.x).start())

    def relation_rows(k):
        at = slice(k * CHUNK, (k + 1) * CHUNK)
        r1[at, :] = onehot(iota((CHUNK, RELPAD), 1) == columns[at, 1:2])
        rt[:, at] = nt(rel[...], r1[at, 0:RELS]).astype(BF16)
    for load in loads[2:6]:
        load.wait()
    ids[...] = jnp.full(ids.shape, -4, I32)
    for k in range(4):
        ids[k : k + 1, 0:SPAN] = raw[k]
    given = ids[...]
    place = lax.bitwise_and(given, 3) * NDOM + lax.shift_right_arithmetic(given, 2)
    ids[...] = jnp.where(iota(ids.shape, 0) == 1, given, place)
    columns = ids[...].T
    loads[6].wait()
    for k in range(SLOTS // CHUNK):
        relation_rows(k)
    times = jnp.zeros((ROWS, 1), F32)
    for k in range(SLOTS // CHUNK):
        at = slice(k * CHUNK, (k + 1) * CHUNK)
        hit = iota((ROWS, CHUNK), 0) == ids[3:4, at]
        times += jnp.sum(jnp.where(hit, 1.0, 0.0), axis=1, keepdims=True)
        h1[:, at] = onehot(iota((ROWS, CHUNK), 0) == ids[0:1, at])
        t1[:, at] = onehot(iota((ROWS, CHUNK), 0) == ids[2:3, at])
    logc[...] = jnp.where(times > 0.0, jnp.log(jnp.maximum(times, 1.0)), NEVER)
    def rows_in(p):
        d, n = PIECES[p]
        arrived(gx.at[pl.ds(0, NX - 1), pl.ds(d, n)], r_3.at[p])
        for x in range(NX):
            lanes = slice(x * NDOM, (x + 1) * NDOM)
            hb[d : d + n, lanes] = gx[x, d : d + n, 0:NDOM]
            tb[d : d + n, lanes] = gx[x, d : d + n, NDOM:]
        tr[:, d : d + n] = tb[d : d + n, :].T
        ht[d : d + n, :] = nn(hb[d : d + n, :], h1[...]).astype(BF16)
        tt[d : d + n, :] = nn(tb[d : d + n, :], t1[...]).astype(BF16)
    over_yc(0)
    over_yc(1)
    over_x(0)
    over_yc(2)
    over_x(1)
    over_x(2)
    rows_in(0)
    rows_in(1)
    rows_in(2)

    def chunk(k, carry):
        at = pl.ds(pl.multiple_of(k * CHUNK, CHUNK), CHUNK)
        h, r, t = ht[:, at].astype(F32), rt[:, at].astype(F32), tt[:, at].astype(F32)
        h_re, h_im = h[0:HALF], h[HALF:D]
        r_re, r_im = r[0:HALF], r[HALF:D]
        q_re = h_re * r_re - h_im * r_im
        q_im = h_re * r_im + h_im * r_re
        s0 = jnp.sum(q_re * t[0:HALF] + q_im * t[HALF:D], axis=0, keepdims=True)
        q_low = jnp.concatenate([q_re, q_im], axis=0).astype(BF16)
        ql[:, at] = q_low
        s = nn(tr[...], q_low) + logc[...]
        m = jnp.maximum(s0, jnp.max(s, axis=0, keepdims=True))
        e0 = jnp.exp(s0 - m)
        e = jnp.exp(s - m)
        z = e0 + jnp.sum(e, axis=0, keepdims=True)
        slot = iota((1, CHUNK), 1) + k * CHUNK
        valid = jnp.where(slot < count[0], 1.0, 0.0)
        g0 = valid * (e0 / z - 1.0)
        tail_hit = iota((ROWS, CHUNK), 0) == ids[2:3, at]
        a = (e * (valid / z) + jnp.where(tail_hit, g0, 0.0)).astype(BF16)
        av[:, at] = a
        dq = nn(tb[...], a)
        d_re, d_im = dq[0:HALF], dq[HALF:D]
        dh[:, at] = jnp.concatenate(
            [d_re * r_re + d_im * r_im, d_im * r_re - d_re * r_im], axis=0
        ).astype(BF16)
        dr[:, at] = jnp.concatenate(
            [d_re * h_re + d_im * h_im, d_im * h_re - d_re * h_im], axis=0
        ).astype(BF16)
        return carry
    lax.fori_loop(0, SLOTS // CHUNK, chunk, 0, unroll=True)

    def ent_copy(p, dst, src):
        part = pl.ds(*BACK[p])
        return remote(es.at[dst, part], rex.at[src, part], s_e, r_e.at[p], me.at(x=dst))

    def b1_copy(p, dst, src):
        return remote(sb1[p].at[dst], rb1[p].at[src], s_b1.at[p], r_b1.at[p], me.at(yc=dst))

    def b2_copy(p, dst, src):
        return remote(sb2[p].at[dst], rb2[p].at[src], s_b2.at[p], r_b2.at[p], me.at(z=dst))

    other_core = me.at(yc=me.y * NC + (1 - me.c))

    def core_copy(j):
        return remote(oc.at[j], rc.at[j], s_c, r_c.at[j], other_core)

    axes = (("y", "x"), ("x", "y"))
    index = {"x": me.x, "y": me.y}

    def copy_a(h, dst, src):
        return remote(asend.at[h, dst], aland.at[h, src], s_a.at[h], r_a.at[h], me.at(**{axes[h][0]: dst}))

    def copy_b(h, dst, src):
        return remote(bsend.at[h, dst], bland.at[h, src], s_b.at[h], r_b.at[h], me.at(**{axes[h][1]: dst}))

    def z_copy(dst, src):
        return remote(zs.at[dst], rz.at[src], s_z.at[dst], r_z, me.at(z=dst))

    def az_copy(dst, src):
        return remote(agz.at[src], agz.at[src], s_az, r_az.at[src], me.at(z=dst))

    def copy_d(h, dst, src):
        part = dback.at[h, src]
        return remote(part, part, s_d.at[h], r_d.at[h], me.at(**{axes[h][1]: dst}))

    def copy_f(h, dst, src):
        part = fback.at[h, src]
        return remote(part, part, s_f.at[h], r_f.at[h, src], me.at(**{axes[h][0]: dst}))

    def copy_g(h, j):
        return remote(fback.at[h, j], gback.at[h, j], s_g.at[h], r_g.at[h], other_core)

    def entity_block(x):
        lanes = pl.ds(pl.multiple_of(x * NDOM, NDOM), NDOM)
        es[x, :, 0:NDOM] = nt(dh[...], h1[lanes, :]).astype(BF16)
        es[x, :, NDOM : 2 * NDOM] = nt(ql[...], av[lanes, :]).astype(BF16)

    def entity_out(x):
        for p in range(NB):
            ent_copy(p, x, me.x).start()

    def relation_block(c, y):
        lanes = pl.ds(pl.multiple_of((c * NY + y) * WIDE, WIDE), WIDE)
        return nn(dr[...], r1[:, lanes])

    def to_core(j):
        oc[j] = relation_block(1 - me.c, j).astype(BF16)
        core_copy(j).start()

    def with_core(j):
        block = relation_block(me.c, j)
        core_copy(j).wait_recv()
        block = (block + rc[j].astype(F32)).astype(BF16)
        for h in range(NH):
            asend[h, j] = block[:, h * LANES : (h + 1) * LANES]

            @pl.when(j != index[axes[h][0]])
            def _(h=h):
                copy_a(h, j, index[axes[h][0]]).start()

    def each(body):
        def step(k, carry):
            body(lax.rem(me.y + k, NY))
            return carry

        lax.fori_loop(1, NY + 1, step, 0)

    def four(ref, h):
        return sum(ref[h, j].astype(F32) for j in range(NY))

    def rel_second(h):
        first, second = axes[h]
        aland[h, index[first]] = asend[h, index[first]]
        arrived(aland.at[h, pl.ds(0, NY - 1)], r_a.at[h])
        total = four(aland, h).astype(BF16)
        for j in range(NX):
            n = min(XROWS, D - j * XROWS)
            bsend[h, j, 0:n] = total[j * XROWS : j * XROWS + n]
            if n < XROWS:
                bsend[h, j, n:] = jnp.zeros((XROWS - n, LANES), BF16)
        me.others(second, lambda q: copy_b(h, q, index[second]).start())

    def tiles(body, parts=range(NH)):
        def step(i, carry):
            z = lax.div(i, XTILES) * 8 + lax.rem(i, XTILES)

            @pl.when(z != me.z)
            def _():
                body(z)

            return carry

        lax.fori_loop(parts[0] * XTILES, (parts[-1] + 1) * XTILES, step, 0)

    def rel_z(h):
        second = axes[h][1]
        bland[h, index[second]] = bsend[h, index[second]]
        arrived(bland.at[h, pl.ds(0, NX - 1)], r_b.at[h])
        zs[h * 8 : h * 8 + XTILES] = four(bland, h).astype(BF16).reshape(XTILES, 16, LANES)
        tiles(lambda q: z_copy(q, me.z).start(), (h,))

    owns = lax.rem(me.z, 8) < XTILES

    def rel_az():
        @pl.when(owns)
        def _():
            rz[me.z] = zs[me.z]
            arrived(rz.at[pl.ds(0, NZ - 1)], r_z)
            total = rz[0].astype(F32)
            for z in range(1, NZ):
                total += rz[z].astype(F32)
            agz[me.z] = total.astype(BF16)
            me.others("z", lambda q: az_copy(q, me.z).start())

    def rel_back1(h):
        second = axes[h][1]
        tiles(lambda q: az_copy(q, q).wait_recv(), (h,))
        dback[h, index[second]] = agz[h * 8 : h * 8 + XTILES].reshape(XROWS, LANES)
        me.others(second, lambda q: copy_d(h, q, index[second]).start())

    def rel_back2(h):
        first = axes[h][0]
        arrived(dback.at[h, pl.ds(0, NX - 1)], r_d.at[h])
        for j in range(NX):
            n = min(XROWS, D - j * XROWS)
            fback[h, index[first], j * XROWS : j * XROWS + n] = dback[h, j, 0:n]
        me.others(first, lambda q: copy_f(h, q, index[first]).start())
        copy_g(h, index[first]).start()

    def rel_core():
        def step(k, carry):
            for h in range(NH):
                j = lax.rem(index[axes[h][0]] + k, NX)
                copy_f(h, j, j).wait_recv()
                copy_g(h, j).start()
            return carry

        lax.fori_loop(1, NX, step, 0)

    def rel_done():
        low = me.c == 0
        for h in range(NH):
            arrived(gback.at[h], r_g.at[h])
            for j in range(NY):
                here, there = fback[h, j].astype(F32), gback[h, j].astype(F32)
                for c in range(NC):
                    start = ((c * NY + j) * NH + h) * LANES
                    n = min(LANES, RELS - start)
                    block = jnp.where(low, here, there) if c == 0 else jnp.where(low, there, here)
                    rel_out[:, start : start + n] = block.astype(BF16)[:, 0:n]

    def ent_yc(p):
        d, n = BACK[p]
        rex[me.x, d : d + n] = es[me.x, d : d + n]
        arrived(rex.at[pl.ds(0, NX - 1), pl.ds(d, n)], r_e.at[p])
        total = sum(rex[x, d : d + n].astype(F32) for x in range(NX)).astype(BF16)
        turned = nt(by_owner(), total).astype(BF16).reshape(NYC, 2 * NZ, n)
        sb1[p][...] = turned
        me.others("yc", lambda q: b1_copy(p, q, me.yc).start())
        rb1[p][me.yc] = sb1[p][me.yc]

    def ent_rows(p):
        arrived(rb1[p].at[pl.ds(0, NYC - 1)], r_b1.at[p])
        turned = tn(swap_zy(), rb1[p][...].reshape(2 * NDOM, BACK[p][1])).astype(BF16)
        sb2[p][...] = turned.reshape(NZ, 2 * NYC, BACK[p][1])
        rb2[p][me.z] = sb2[p][me.z]

    def ent_z(p):
        me.others("z", lambda q: b2_copy(p, q, me.z).start())

    def ent_done(p, pick):
        d, n = BACK[p]
        arrived(rb2[p].at[pl.ds(0, NZ - 1)], r_b2.at[p])
        ent_out[d : d + n, :] = tn(rb2[p][...].reshape(2 * NDOM, n), pick).astype(BF16)
    each(to_core)
    each(with_core)
    me.others("x", entity_block)
    entity_block(me.x)
    parts = jnp.concatenate([onehot(iota(sq, 0) == plan[h : h + 1, :]) for h in range(2)], axis=1)
    pick = nt(by_send_order(), parts).astype(BF16)
    for h in range(NH):
        rel_second(h)
    me.others("x", entity_out)
    for h in range(NH):
        rel_z(h)
    for p in range(NB):
        ent_yc(p)
    rel_az()
    for p in range(NB):
        ent_rows(p)
        ent_z(p)
    for h in range(NH):
        rel_back1(h)
    for h in range(NH):
        rel_back2(h)
    rel_core()
    for p in range(NB):
        ent_done(p, pick)
    rel_done()
    arrived(gx.at[pl.ds(0, NX - 1)], s_3)
    arrived(es.at[pl.ds(0, NX - 1)], s_e)
    for p in range(NP):
        arrived(snd1[p].at[pl.ds(0, NZ - 1)], s_1.at[p])
        arrived(snd2[p].at[pl.ds(0, NYC - 1)], s_2.at[p])
    for p in range(NB):
        arrived(sb1[p].at[pl.ds(0, NYC - 1)], s_b1.at[p])
        arrived(sb2[p].at[pl.ds(0, NZ - 1)], s_b2.at[p])
    arrived(oc, s_c)
    for h in range(NH):
        arrived(asend.at[h, pl.ds(0, NY - 1)], s_a.at[h])
        arrived(bsend.at[h, pl.ds(0, NX - 1)], s_b.at[h])
        arrived(dback.at[h, pl.ds(0, NX - 1)], s_d.at[h])
        arrived(fback.at[h, pl.ds(0, NY - 1)], s_f.at[h])
        arrived(gback.at[h], s_g.at[h])
    tiles(lambda q: z_copy(q, me.z).wait_send())

    @pl.when(owns)
    def _():
        arrived(agz.at[pl.ds(0, NZ - 1)], s_az)


def scratch():
    def bf16(*shape):
        return pltpu.VMEM(shape, BF16)

    dma = pltpu.SemaphoreType.DMA

    def rows(pieces, *lead):
        return tuple(bf16(*lead, n) for _, n in pieces)

    by_z, by_yc = rows(PIECES, NZ, 2 * NYC), rows(PIECES, NYC, 2 * NZ)
    back_z, back_yc = rows(BACK, NZ, 2 * NYC), rows(BACK, NYC, 2 * NZ)
    block, slots, tile = bf16(NX, D, WIDE), bf16(D, SLOTS), bf16(NZ, 16, LANES)
    half, thin = bf16(NH, NY, D, LANES), bf16(NH, NX, XROWS, LANES)
    hops = [dma((NP,)), dma((NP,))]
    sides = [dma((NH,)), dma((NH,))]
    return (
        [bf16(D, NDOM), bf16(D, RELS), pltpu.VMEM((2, NDOM), I32)]
        + [pltpu.VMEM((4, 1, SPAN), I32), pltpu.VMEM((8, SLOTS), I32)]
        + [by_z, by_z, by_yc, by_yc, block]
        + [bf16(D, ROWS), bf16(D, ROWS), bf16(ROWS, D), pltpu.VMEM((ROWS, 1), F32)]
        + [bf16(ROWS, SLOTS), bf16(ROWS, SLOTS), bf16(SLOTS, RELPAD)]
        + [slots, slots, slots, slots, slots, bf16(ROWS, SLOTS), slots]
        + [block, block, back_yc, back_yc, back_z, back_z]
        + [block, block, half, half, thin, thin, tile, tile, tile, thin, half, half]
        + [dma((7,))]
        + hops * 2
        + [dma, dma((NP,)), dma, dma((NB,))]
        + [dma((NB,))] * 4
        + [dma, dma((NY,))]
        + sides * 2
        + [dma((NZ,)), dma, dma, dma((NZ,))]
        + sides
        + [dma((NH,)), dma((NH, NY))]
        + sides
    )


def per_device(entity, relation, head_ids, relation_ids, tail_ids, negative_ids, span_counts, plan):
    ent_out, rel_out = pl.pallas_call(
        kernel,
        out_shape=(
            jax.ShapeDtypeStruct((D, NDOM), BF16),
            jax.ShapeDtypeStruct((D, RELS), BF16),
        ),
        in_specs=[pl.BlockSpec(memory_space=pltpu.SMEM)] + [HBM] * 7,
        out_specs=(VMEM, VMEM),
        scratch_shapes=scratch(),
        compiler_params=pltpu.CompilerParams(
            collective_id=0, has_side_effects=True, vmem_limit_bytes=40 << 20
        ),
        name="bucket_round",
    )(
        span_counts,
        *(
            pltpu.with_memory_space_constraint(v, pltpu.HBM)
            for v in (
                jnp.transpose(entity, (1, 2, 0)),
                relation.T,
                head_ids.reshape(1, SPAN),
                relation_ids.reshape(1, SPAN),
                tail_ids.reshape(1, SPAN),
                negative_ids,
                plan.T,
            )
        ),
    )
    return jnp.transpose(ent_out.reshape(1, D, NDOM), (2, 0, 1)), rel_out.T


def solution(mesh):
    placed = (
        P(None, "dom", None),
        P(),
        P(("dom", "rep")),
        P(("dom", "rep")),
        P(("dom", "rep")),
        P(("dom", "rep"), None),
        P(("dom", "rep")),
        P(),
    )
    return jax.shard_map(
        per_device,
        mesh=mesh,
        in_specs=placed,
        out_specs=(P(None, ("dom", "rep"), None), P()),
        check_vma=False,
    )
```

time: 103 us -> 94.7 us (0.919)
  Pallas kernels: 99.8 us -> 91.5 us
    pallas_call x1, Pallas kernels: 99.8 us -> 91.5 us  [per_device(): pl.pallas_call(kernel, out_shape=(jax.ShapeDtypeStruct((D, NDOM), BF16),...]
where the time goes in v3:
time: 94.7 us; the launch traced here: 94.6 us
  Pallas kernels  91.5 us (97%)
  local copies, waits for them, and re-layouts  1.81 us (2%)
  between operations  1.29 us (1%)
    pallas_call x1, Pallas kernels, per_device(): pl.pallas_call(kernel, out_shape=(jax.ShapeDtypeStruct((D, NDOM), BF16),...  91.5 us

profile of v3, /device:TPU:1, one launch (start us, length us, event | category | flops | bytes accessed | tf_op | source)
XLA Modules:
  0.0 94.6 jit_solution(11991297718066570054)
XLA Ops:
  1.3 91.5 %bucket_round.1 = (bf16[400,128]{1,0:T(8,128)(2,1)S(1)}, bf16[400,2000]{1,0:T(8,128)(2,1)S(1)}) custom-call(s32[1]{0:T(128)S(6)} %copy.12.count, bf16[4,400,128]{2,1,0:T(8,128)(2,1)} %bitcast.13, bf16[400,2000]{1,0:T(8,128)(2,1)} %bitcast.12, s32[1,1000]{1,0:T(1,128)} %bitcast.14, s32[1,1000]{1,0:T(1,128)} %bitcast.15, s32[1,1000]{1,0:T(1,128)} %bitcast.16, ...), custom_call_target="tpu_custom_call" | custom-call | tf_op jit(solution)/shard_map/bucket_round/pallas_call | solution.py:533
  92.8 0.6 copy.13
  93.4 1.2 %copy.14 = bf16[2000,400]{0,1:T(8,128)(2,1)} copy(bf16[2000,400]{0,1:T(8,128)(2,1)S(1)} %bitcast.10) | data formatting | bytes 3200000

commit v4 on v3

--- a/solution.py
+++ b/solution.py
@@ -19,7 +19,7 @@
 RELPAD = 2048
 SPAN = 1000
 SLOTS = 1024
-CHUNK = 256
+CHUNK = 1024
 ROWS = 512
 WIDE = 256
 PIECES = ((0, 256), (256, 128), (384, 16))
@@ -154,9 +154,9 @@
     sq = (NDOM, NDOM)
     plan_hit = jnp.concatenate([onehot(iota(sq, 0) == plan[h : h + 1, :]) for h in range(2)], axis=1)
     picked = nn(stripe[...], plan_hit).astype(BF16)
-    rows = nt(by_send_order(), picked).astype(BF16)
+    rows = nt(by_owner(), picked).astype(BF16)
     for p, (d, n) in enumerate(PIECES):
-        snd1[p][...] = rows[:, d : d + n].reshape(NZ, 2 * NYC, n)
+        snd2[p][...] = rows[:, d : d + n].reshape(NYC, 2 * NZ, n)
 
     def copy1(p, dst, src):
         return remote(snd1[p].at[dst], rcv1[p].at[src], s_1.at[p], r_1.at[p], me.at(z=dst))
@@ -169,20 +169,20 @@
         return remote(part, part, s_3, r_3.at[p], me.at(x=dst))
     pl.semaphore_wait(hello, NX + NYC + NZ - 3)
     for p in range(NP):
-        me.others("z", lambda q, p=p: copy1(p, q, me.z).start())
+        me.others("yc", lambda q, p=p: copy2(p, q, me.yc).start())
+        rcv2[p][me.yc] = snd2[p][me.yc]
+
+    def over_z(p):
+        arrived(rcv2[p].at[pl.ds(0, NYC - 1)], r_2.at[p])
+        turned = tn(swap_zy(), rcv2[p][...].reshape(2 * NDOM, PIECES[p][1])).astype(BF16)
+        snd1[p][...] = turned.reshape(NZ, 2 * NYC, PIECES[p][1])
+        me.others("z", lambda q: copy1(p, q, me.z).start())
         rcv1[p][me.z] = snd1[p][me.z]
-
-    def over_yc(p):
-        arrived(rcv1[p].at[pl.ds(0, NZ - 1)], r_1.at[p])
-        turned = nn(swap_zy(), rcv1[p][...].reshape(2 * NDOM, PIECES[p][1])).astype(BF16)
-        snd2[p][...] = turned.reshape(NYC, 2 * NZ, PIECES[p][1])
-        me.others("yc", lambda q: copy2(p, q, me.yc).start())
-        rcv2[p][me.yc] = snd2[p][me.yc]
 
     def over_x(p):
         d, n = PIECES[p]
-        arrived(rcv2[p].at[pl.ds(0, NYC - 1)], r_2.at[p])
-        turned = tn(rcv2[p][...].reshape(2 * NDOM, n), by_owner()).astype(BF16)
+        arrived(rcv1[p].at[pl.ds(0, NZ - 1)], r_1.at[p])
+        turned = tn(rcv1[p][...].reshape(2 * NDOM, n), by_send_order()).astype(BF16)
         gx[me.x, d : d + n] = turned
         me.others("x", lambda q: copy3(p, q, me.x).start())
 
@@ -190,6 +190,9 @@
         at = slice(k * CHUNK, (k + 1) * CHUNK)
         r1[at, :] = onehot(iota((CHUNK, RELPAD), 1) == columns[at, 1:2])
         rt[:, at] = nt(rel[...], r1[at, 0:RELS]).astype(BF16)
+    over_z(0)
+    over_z(1)
+    over_z(2)
     for load in loads[2:6]:
         load.wait()
     ids[...] = jnp.full(ids.shape, -4, I32)
@@ -220,10 +223,7 @@
         tr[:, d : d + n] = tb[d : d + n, :].T
         ht[d : d + n, :] = nn(hb[d : d + n, :], h1[...]).astype(BF16)
         tt[d : d + n, :] = nn(tb[d : d + n, :], t1[...]).astype(BF16)
-    over_yc(0)
-    over_yc(1)
     over_x(0)
-    over_yc(2)
     over_x(1)
     over_x(2)
     rows_in(0)
@@ -370,7 +370,12 @@
         bland[h, index[second]] = bsend[h, index[second]]
         arrived(bland.at[h, pl.ds(0, NX - 1)], r_b.at[h])
         zs[h * 8 : h * 8 + XTILES] = four(bland, h).astype(BF16).reshape(XTILES, 16, LANES)
-        tiles(lambda q: z_copy(q, me.z).start(), (h,))
+        def to_owner(q):
+            @pl.when(jnp.logical_and(lax.div(q, 8) == h, lax.rem(q, 8) < XTILES))
+            def _():
+                z_copy(q, me.z).start()
+
+        me.others("z", to_owner)
 
     owns = lax.rem(me.z, 8) < XTILES
 
@@ -461,15 +466,16 @@
     rel_az()
     for p in range(NB):
         ent_rows(p)
-        ent_z(p)
     for h in range(NH):
         rel_back1(h)
+    for p in range(NB):
+        ent_z(p)
     for h in range(NH):
         rel_back2(h)
     rel_core()
+    rel_done()
     for p in range(NB):
         ent_done(p, pick)
-    rel_done()
     arrived(gx.at[pl.ds(0, NX - 1)], s_3)
     arrived(es.at[pl.ds(0, NX - 1)], s_e)
     for p in range(NP):

time: 94.7 us -> 90.6 us (0.957)
  Pallas kernels: 91.5 us -> 87.4 us
    pallas_call x1, Pallas kernels: 91.5 us -> 87.4 us  [per_device(): pl.pallas_call(kernel, out_shape=(jax.ShapeDtypeStruct((D, NDOM), BF16),...]
where the time goes in v4:
time: 90.6 us; the launch traced here: 90.5 us
  Pallas kernels  87.4 us (96%)
  local copies, waits for them, and re-layouts  1.81 us (2%)
  between operations  1.29 us (1%)
    pallas_call x1, Pallas kernels, per_device(): pl.pallas_call(kernel, out_shape=(jax.ShapeDtypeStruct((D, NDOM), BF16),...  87.4 us

profile of v4, /device:TPU:1, one launch (start us, length us, event | category | flops | bytes accessed | tf_op | source)
XLA Modules:
  0.0 90.5 jit_solution(436936692903310362)
XLA Ops:
  1.3 87.4 %bucket_round.1 = (bf16[400,128]{1,0:T(8,128)(2,1)S(1)}, bf16[400,2000]{1,0:T(8,128)(2,1)S(1)}) custom-call(s32[1]{0:T(128)S(6)} %copy.12.count, bf16[4,400,128]{2,1,0:T(8,128)(2,1)} %bitcast.13, bf16[400,2000]{1,0:T(8,128)(2,1)} %bitcast.12, s32[1,1000]{1,0:T(1,128)} %bitcast.14, s32[1,1000]{1,0:T(1,128)} %bitcast.15, s32[1,1000]{1,0:T(1,128)} %bitcast.16, ...), custom_call_target="tpu_custom_call" | custom-call | tf_op jit(solution)/shard_map/bucket_round/pallas_call | solution.py:539
  88.7 0.6 copy.13
  89.3 1.2 %copy.14 = bf16[2000,400]{0,1:T(8,128)(2,1)} copy(bf16[2000,400]{0,1:T(8,128)(2,1)S(1)} %bitcast.10) | data formatting | bytes 3200000

commit v5 on v4

--- a/solution.py
+++ b/solution.py
@@ -144,10 +144,10 @@
         pltpu.make_async_copy(neg_hbm, raw.at[3], s_in.at[5]),
         pltpu.make_async_copy(rel_hbm, rel, s_in.at[6]),
     ]
+    hello = pltpu.get_barrier_semaphore()
+    me.greet(hello)
     for load in loads:
         load.start()
-    hello = pltpu.get_barrier_semaphore()
-    me.greet(hello)
 
     loads[0].wait()
     loads[1].wait()
@@ -456,9 +456,9 @@
     entity_block(me.x)
     parts = jnp.concatenate([onehot(iota(sq, 0) == plan[h : h + 1, :]) for h in range(2)], axis=1)
     pick = nt(by_send_order(), parts).astype(BF16)
-    for h in range(NH):
-        rel_second(h)
+    rel_second(0)
     me.others("x", entity_out)
+    rel_second(1)
     for h in range(NH):
         rel_z(h)
     for p in range(NB):

time: 90.6 us -> 90.5 us (level)
  no operation moved by 1% of the time
where the time goes in v5:
time: 90.5 us; the launch traced here: 90.4 us
  Pallas kernels  87.3 us (96%)
  local copies, waits for them, and re-layouts  1.81 us (2%)
  between operations  1.29 us (1%)
    pallas_call x1, Pallas kernels, per_device(): pl.pallas_call(kernel, out_shape=(jax.ShapeDtypeStruct((D, NDOM), BF16),...  87.3 us

profile of v5, /device:TPU:1, one launch (start us, length us, event | category | flops | bytes accessed | tf_op | source)
XLA Modules:
  0.0 90.4 jit_solution(670231069810136291)
XLA Ops:
  1.3 87.3 %bucket_round.1 = (bf16[400,128]{1,0:T(8,128)(2,1)S(1)}, bf16[400,2000]{1,0:T(8,128)(2,1)S(1)}) custom-call(s32[1]{0:T(128)S(6)} %copy.12.count, bf16[4,400,128]{2,1,0:T(8,128)(2,1)} %bitcast.13, bf16[400,2000]{1,0:T(8,128)(2,1)} %bitcast.12, s32[1,1000]{1,0:T(1,128)} %bitcast.14, s32[1,1000]{1,0:T(1,128)} %bitcast.15, s32[1,1000]{1,0:T(1,128)} %bitcast.16, ...), custom_call_target="tpu_custom_call" | custom-call | tf_op jit(solution)/shard_map/bucket_round/pallas_call | solution.py:539
  88.6 0.6 copy.13
  89.2 1.2 %copy.14 = bf16[2000,400]{0,1:T(8,128)(2,1)} copy(bf16[2000,400]{0,1:T(8,128)(2,1)S(1)} %bitcast.10) | data formatting | bytes 3200000

commit v6 on v5

--- a/solution.py
+++ b/solution.py
@@ -24,7 +24,7 @@
 WIDE = 256
 PIECES = ((0, 256), (256, 128), (384, 16))
 NP = len(PIECES)
-BACK = ((0, 256), (256, 144))
+BACK = ((0, 400),)
 NB = len(BACK)
 NH = 2
 LANES = 128

time: 90.5 us -> 90.6 us (level)
  no operation moved by 1% of the time
where the time goes in v6:
time: 90.6 us; the launch traced here: 90.4 us
  Pallas kernels  87.4 us (96%)
  local copies, waits for them, and re-layouts  1.81 us (2%)
  between operations  1.29 us (1%)
    pallas_call x1, Pallas kernels, per_device(): pl.pallas_call(kernel, out_shape=(jax.ShapeDtypeStruct((D, NDOM), BF16),...  87.4 us

profile of v6, /device:TPU:1, one launch (start us, length us, event | category | flops | bytes accessed | tf_op | source)
XLA Modules:
  0.0 90.4 jit_solution(14478842335272415609)
XLA Ops:
  1.3 87.4 %bucket_round.1 = (bf16[400,128]{1,0:T(8,128)(2,1)S(1)}, bf16[400,2000]{1,0:T(8,128)(2,1)S(1)}) custom-call(s32[1]{0:T(128)S(6)} %copy.12.count, bf16[4,400,128]{2,1,0:T(8,128)(2,1)} %bitcast.13, bf16[400,2000]{1,0:T(8,128)(2,1)} %bitcast.12, s32[1,1000]{1,0:T(1,128)} %bitcast.14, s32[1,1000]{1,0:T(1,128)} %bitcast.15, s32[1,1000]{1,0:T(1,128)} %bitcast.16, ...), custom_call_target="tpu_custom_call" | custom-call | tf_op jit(solution)/shard_map/bucket_round/pallas_call | solution.py:539
  88.6 0.6 copy.13
  89.3 1.2 %copy.14 = bf16[2000,400]{0,1:T(8,128)(2,1)} copy(bf16[2000,400]{0,1:T(8,128)(2,1)S(1)} %bitcast.10) | data formatting | bytes 3200000
